TPU v7x, 256 devices: a whole 4x4x8 slice. The times are simulated.
256 devices in a mesh: dp: 4 (over x_lo, core), blk: 64 (over x_hi, z, y).
Axes of the slice: x: 4 (x_hi: 2, x_lo: 2; x = x_hi * 2 + x_lo), y: 4, z: 8, core: 2. Of those that a mesh axis runs over, the one named last changes fastest.
Arguments:
- tokens: bfloat16 [65536, 3072], P(('dp', 'blk')), may hold values from -6 to 6
- cotangent: bfloat16 [65536, 3072], P(('dp', 'blk')), may hold values from -6 to 6
- norm_gain: float32 [3072], replicated, may hold values from 0.1 to 1.9
- gate_weight: bfloat16 [3072, 8192], P(None, 'blk'), may hold values from -0.109375 to 0.109375
- up_weight: bfloat16 [3072, 8192], P(None, 'blk'), may hold values from -0.109375 to 0.109375
- down_weight: bfloat16 [8192, 3072], P('blk'), may hold values from -0.0625 to 0.0625
Outputs:
- block_out: bfloat16 [65536, 3072], P(('dp', 'blk'))
- input_grad: bfloat16 [65536, 3072], P(('dp', 'blk'))
- gate_grad: float32 [3072, 8192], P('dp', 'blk')
- up_grad: float32 [3072, 8192], P('dp', 'blk')
- down_grad: float32 [8192, 3072], P('blk', 'dp')
All inputs are finite; a program needn't handle non-finite values.
Results may differ from a plain program's by a relative error of at most 0.006.
Values may be sent and summed in bfloat16 or wider, within the bound.
No kernel may reach another device: no remote copies, remote signals or barrier semaphores. Data moves between devices by JAX's collectives and lax.ppermute only.
A program may use at most 128 MiB of HBM per device.

v0:
```python
import jax
import jax.numpy as jnp
from jax import lax
from jax.sharding import PartitionSpec as P

HOPS = 3


epsilon = 1e-05
grad_scale = 0.0625


def from_behind(value, axis, steps):
    count = lax.axis_size(axis)
    pairs = [(source, (source + steps) % count) for source in range(count)]
    return lax.ppermute(value, axis, pairs)


def shards(tokens, cotangent, norm_gain, gate_weight, up_weight, down_weight):
    contract_rows = (((0,), (0,)), ((), ()))
    contract_cols = (((1,), (1,)), ((), ()))
    wide = tokens.astype(jnp.float32)
    inverse = lax.rsqrt(jnp.mean(wide * wide, axis=-1, keepdims=True) + epsilon)
    normed = (wide * inverse * norm_gain).astype(jnp.bfloat16)
    weights = (gate_weight, up_weight, down_weight)
    mlp_total = jnp.zeros(tokens.shape, jnp.float32)
    dnormed = jnp.zeros(tokens.shape, jnp.float32)
    terms = []
    for hop_index in range(HOPS):
        if hop_index > 0:
            weights = from_behind((weights[0], weights[1], weights[2]), "blk", 1)
        gate_part, up_part, down_part = weights
        pre_gate = jnp.dot(normed, gate_part, preferred_element_type=jnp.float32)
        pre_up = jnp.dot(normed, up_part, preferred_element_type=jnp.float32)
        sigmoid_gate = jax.nn.sigmoid(pre_gate)
        active = pre_gate * sigmoid_gate
        hidden = (active * pre_up).astype(jnp.bfloat16)
        mlp_total = mlp_total + jnp.dot(hidden, down_part, preferred_element_type=jnp.float32)
        hidden_grad = lax.dot_general(
            cotangent, down_part, contract_cols, preferred_element_type=jnp.float32
        )
        gate_delta = (
            hidden_grad * pre_up * sigmoid_gate * (1.0 + pre_gate * (1.0 - sigmoid_gate))
        ).astype(jnp.bfloat16)
        up_delta = (hidden_grad * active).astype(jnp.bfloat16)
        both_deltas = jnp.concatenate([gate_delta, up_delta], axis=1)
        both_parts = jnp.concatenate([gate_part, up_part], axis=1)
        dnormed = dnormed + lax.dot_general(
            both_deltas, both_parts, contract_cols, preferred_element_type=jnp.float32
        )
        gate_term = lax.dot_general(
            normed, gate_delta, contract_rows, preferred_element_type=jnp.float32
        )
        up_term = lax.dot_general(
            normed, up_delta, contract_rows, preferred_element_type=jnp.float32
        )
        down_term = lax.dot_general(
            cotangent, hidden, contract_rows, preferred_element_type=jnp.float32
        )
        terms.append(jnp.stack([gate_term, up_term, down_term]))
    block_out = (wide + mlp_total).astype(jnp.bfloat16)
    scaled = wide * inverse
    along = dnormed * norm_gain
    norm_back = inverse * (along - scaled * jnp.mean(along * scaled, axis=-1, keepdims=True))
    input_grad = (cotangent.astype(jnp.float32) + norm_back).astype(jnp.bfloat16)
    carried = terms[0]
    for hop_index in range(1, HOPS):
        carried = from_behind(carried, "blk", 1) + terms[hop_index]
    carried = from_behind(carried, "blk", 1 - HOPS)
    carried = lax.psum_scatter(carried, "dp", scatter_dimension=1, tiled=True)
    carried = carried * grad_scale
    return (block_out, input_grad, carried[0], carried[1], jnp.transpose(carried[2]))


def solution(mesh):
    in_specs = (
        P(("dp", "blk"), None),
        P(("dp", "blk"), None),
        P(),
        P(None, "blk"),
        P(None, "blk"),
        P("blk", None),
    )
    out_specs = (
        P(("dp", "blk"), None),
        P(("dp", "blk"), None),
        P("dp", "blk"),
        P("dp", "blk"),
        P("blk", "dp"),
    )
    return jax.shard_map(shards, mesh=mesh, in_specs=in_specs, out_specs=out_specs, check_vma=False)
```

profile of v0, /device:TPU:2, one launch (start us, length us, event | category | flops | bytes accessed | tf_op | source)
XLA Modules:
  0.0 505.4 jit_solution(4477673325689574467)
XLA Ops:
  7.2 1.9 fusion.11
  9.2 1.9 fusion.41
  12.2 0.7 fusion.37
  13.4 0.7 multiply_convert_fusion.5
  14.1 0.7 convolution_bitcast_fusion.6
  16.4 1.6 collective-permute-start.6
  18.1 1.6 collective-permute-start.2
  19.6 1.3 collective-permute-start.1
  20.9 1.6 collective-permute-start
  22.5 123.3 %collective-permute-done.2 = bf16[128,3072]{1,0:T(8,128)(2,1)S(1)} collective-permute-done((bf16[128,3072]{1,0:T(8,128)(2,1)S(1)}, bf16[128,3072]{1,0:T(8,128)(2,1)S(1)}, u32[]{:S(2)}, u32[]{:S(2)}) %collective-permute-start.2) | collective-permute-done | bytes 786464 | tf_op jit(solution)/shard_map/ppermute | solution.py:16
  145.9 0.7 fusion.42
  146.5 16.2 %collective-permute-done.1 = bf16[3072,128]{1,0:T(8,128)(2,1)S(1)} collective-permute-done((bf16[3072,128]{1,0:T(8,128)(2,1)S(1)}, bf16[3072,128]{1,0:T(8,128)(2,1)S(1)}, u32[]{:S(2)}, u32[]{:S(2)}) %collective-permute-start.1) | collective-permute-done | bytes 786464 | tf_op jit(solution)/shard_map/ppermute | solution.py:16
  162.7 0.7 fusion.39
  163.4 15.4 %collective-permute-done = bf16[3072,128]{1,0:T(8,128)(2,1)S(1)} collective-permute-done((bf16[3072,128]{1,0:T(8,128)(2,1)S(1)}, bf16[3072,128]{1,0:T(8,128)(2,1)S(1)}, u32[]{:S(2)}, u32[]{:S(2)}) %collective-permute-start) | collective-permute-done | bytes 786464 | tf_op jit(solution)/shard_map/ppermute | solution.py:16
  178.7 0.7 multiply_convert_fusion.3
  179.4 0.7 convolution_bitcast_fusion.3
  182.5 126.8 %collective-permute-done.5 = bf16[128,3072]{1,0:T(8,128)(2,1)S(1)} collective-permute-done((bf16[128,3072]{1,0:T(8,128)(2,1)S(1)}, bf16[128,3072]{1,0:T(8,128)(2,1)S(1)}, u32[]{:S(2)}, u32[]{:S(2)}) %collective-permute-start.5) | collective-permute-done | bytes 786464 | tf_op jit(solution)/shard_map/ppermute | solution.py:16
  309.3 0.7 fusion.43
  310.0 16.2 %collective-permute-done.4 = bf16[3072,128]{1,0:T(8,128)(2,1)S(1)} collective-permute-done((bf16[3072,128]{1,0:T(8,128)(2,1)S(1)}, bf16[3072,128]{1,0:T(8,128)(2,1)S(1)}, u32[]{:S(2)}, u32[]{:S(2)}) %collective-permute-start.4) | collective-permute-done | bytes 786464 | tf_op jit(solution)/shard_map/ppermute | solution.py:16
  326.9 14.4 %collective-permute-done.3 = bf16[3072,128]{1,0:T(8,128)(2,1)S(1)} collective-permute-done((bf16[3072,128]{1,0:T(8,128)(2,1)S(1)}, bf16[3072,128]{1,0:T(8,128)(2,1)S(1)}, u32[]{:S(2)}, u32[]{:S(2)}) %collective-permute-start.3) | collective-permute-done | bytes 786464 | tf_op jit(solution)/shard_map/ppermute | solution.py:16
  341.3 0.7 multiply_convert_fusion.1
  342.0 0.7 convolution_bitcast_fusion
  344.7 103.7 %collective-permute-done.8 = f32[3,3072,128]{2,1,0:T(8,128)} collective-permute-done((f32[3,3072,128]{2,1,0:T(8,128)S(1)}, f32[3,3072,128]{2,1,0:T(8,128)}, u32[]{:S(2)}, u32[]{:S(2)}) %collective-permute-start.8) | collective-permute-done | bytes 4718624 | tf_op jit(solution)/shard_map/ppermute | solution.py:16
  448.4 2.1 fusion.12
  451.8 0.7 convolution_add_fusion.1
  454.3 1.1 fusion.6
  455.5 1.8 fusion.4
  457.3 2.3 fusion.10
  459.6 35.8 %reduce-scatter.2.cloned.1.call-done = f32[3,768,128]{2,1,0:T(8,128)} async-done(((f32[3,3072,128]{2,1,0:T(8,128)}), f32[3,768,128]{2,1,0:T(8,128)}) %reduce-scatter.2.cloned.1.call-update) | async-done | bytes 1179664 | tf_op jit(solution)/shard_map/reduce_scatter | solution.py:70
  495.4 1.3 broadcast_multiply_fusion
  496.7 1.0 slice_bitcast_fusion
  497.7 0.9 copy.14
  (74 shorter events, 11.1 us)
Async XLA Ops:
  7.2 2.0 copy-start
  7.2 488.2 %reduce-scatter.2.cloned.1.call-start = ((), (), s32[]{:S(2)}) async-start(), calls=%async_computation.1 | async-start | bytes 5898240 | tf_op jit(solution)/shard_map/reduce_scatter | solution.py:70
  9.1 2.0 copy-start.1
  9.1 2.0 copy-start.24
  11.1 1.1 copy-start.2
  12.2 1.1 copy-start.9
  16.1 2.0 copy-start.12
  16.4 165.0 %collective-permute-start.6 = (f32[3,3072,128]{2,1,0:T(8,128)S(1)}, f32[3,3072,128]{2,1,0:T(8,128)S(1)}, u32[]{:S(2)}, u32[]{:S(2)}) collective-permute-start(f32[3,3072,128]{2,1,0:T(8,128)S(1)} %pad_maximum_fusion), channel_id=1, source_target_pairs={{0,1},{1,2},{2,3},{3,4},{4,5},{5,6},{6,7},{7,8},{8,9},{9,10},{10,1... | collective-permute-start | bytes 14155784 | tf_op jit(solution)/shard_map/ppermute | solution.py:16
  18.1 127.8 %collective-permute-start.2 = (bf16[128,3072]{1,0:T(8,128)(2,1)S(1)}, bf16[128,3072]{1,0:T(8,128)(2,1)S(1)}, u32[]{:S(2)}, u32[]{:S(2)}) collective-permute-start(bf16[128,3072]{1,0:T(8,128)(2,1)S(1)} %copy-done.12), channel_id=1, source_target_pairs={{0,1},{1,2},{2,3},{3,4},{4,5},{5,6},{6,7},{7,8},{8,9},{9,10},{10,1... | collective-permute-start | bytes 2359304 | tf_op jit(solution)/shard_map/ppermute | solution.py:16
  19.6 143.1 %collective-permute-start.1 = (bf16[3072,128]{1,0:T(8,128)(2,1)S(1)}, bf16[3072,128]{1,0:T(8,128)(2,1)S(1)}, u32[]{:S(2)}, u32[]{:S(2)}) collective-permute-start(bf16[3072,128]{1,0:T(8,128)(2,1)S(1)} %copy-done.2), channel_id=1, source_target_pairs={{0,1},{1,2},{2,3},{3,4},{4,5},{5,6},{6,7},{7,8},{8,9},{9,10},{10,1... | collective-permute-start | bytes 2359304 | tf_op jit(solution)/shard_map/ppermute | solution.py:16
  20.9 157.8 %collective-permute-start = (bf16[3072,128]{1,0:T(8,128)(2,1)S(1)}, bf16[3072,128]{1,0:T(8,128)(2,1)S(1)}, u32[]{:S(2)}, u32[]{:S(2)}) collective-permute-start(bf16[3072,128]{1,0:T(8,128)(2,1)S(1)} %copy-done.9), channel_id=1, source_target_pairs={{0,1},{1,2},{2,3},{3,4},{4,5},{5,6},{6,7},{7,8},{8,9},{9,10},{10,1... | collective-permute-start | bytes 2359304 | tf_op jit(solution)/shard_map/ppermute | solution.py:16
  145.8 36.2 %copy-start.3 = (bf16[128,3072]{1,0:T(8,128)(2,1)}, bf16[128,3072]{1,0:T(8,128)(2,1)S(1)}, u32[]{:S(2)}) copy-start(bf16[128,3072]{1,0:T(8,128)(2,1)S(1)} %collective-permute-done.2) | copy-start | bytes 2359300
  162.7 19.6 %copy-start.14 = (bf16[3072,128]{1,0:T(8,128)(2,1)}, bf16[3072,128]{1,0:T(8,128)(2,1)S(1)}, u32[]{:S(2)}) copy-start(bf16[3072,128]{1,0:T(8,128)(2,1)S(1)} %collective-permute-done.1) | copy-start | bytes 2359300
  178.7 3.7 copy-start.16
  181.9 162.2 %collective-permute-start.7 = (f32[3,3072,128]{2,1,0:T(8,128)S(1)}, f32[3,3072,128]{2,1,0:T(8,128)S(1)}, u32[]{:S(2)}, u32[]{:S(2)}) collective-permute-start(f32[3,3072,128]{2,1,0:T(8,128)S(1)} %maximum_add_fusion), channel_id=1, source_target_pairs={{0,1},{1,2},{2,3},{3,4},{4,5},{5,6},{6,7},{7,8},{8,9},{9,10},{10,1... | collective-permute-start | bytes 14155784 | tf_op jit(solution)/shard_map/ppermute | solution.py:16
  182.0 127.3 %collective-permute-start.5 = (bf16[128,3072]{1,0:T(8,128)(2,1)S(1)}, bf16[128,3072]{1,0:T(8,128)(2,1)S(1)}, u32[]{:S(2)}, u32[]{:S(2)}) collective-permute-start(bf16[128,3072]{1,0:T(8,128)(2,1)S(1)} %collective-permute-done.2), channel_id=1, source_target_pairs={{0,1},{1,2},{2,3},{3,4},{4,5},{5,6},{6,7},{7,8},{8,9},{9,10},{10,1... | collective-permute-start | bytes 2359304 | tf_op jit(solution)/shard_map/ppermute | solution.py:16
  182.3 143.9 %collective-permute-start.4 = (bf16[3072,128]{1,0:T(8,128)(2,1)S(1)}, bf16[3072,128]{1,0:T(8,128)(2,1)S(1)}, u32[]{:S(2)}, u32[]{:S(2)}) collective-permute-start(bf16[3072,128]{1,0:T(8,128)(2,1)S(1)} %collective-permute-done.1), channel_id=1, source_target_pairs={{0,1},{1,2},{2,3},{3,4},{4,5},{5,6},{6,7},{7,8},{8,9},{9,10},{10,1... | collective-permute-start | bytes 2359304 | tf_op jit(solution)/shard_map/ppermute | solution.py:16
  182.4 158.9 %collective-permute-start.3 = (bf16[3072,128]{1,0:T(8,128)(2,1)S(1)}, bf16[3072,128]{1,0:T(8,128)(2,1)S(1)}, u32[]{:S(2)}, u32[]{:S(2)}) collective-permute-start(bf16[3072,128]{1,0:T(8,128)(2,1)S(1)} %collective-permute-done), channel_id=1, source_target_pairs={{0,1},{1,2},{2,3},{3,4},{4,5},{5,6},{6,7},{7,8},{8,9},{9,10},{10,1... | collective-permute-start | bytes 2359304 | tf_op jit(solution)/shard_map/ppermute | solution.py:16
  309.3 17.5 %copy-start.5 = (bf16[128,3072]{1,0:T(8,128)(2,1)}, bf16[128,3072]{1,0:T(8,128)(2,1)S(1)}, u32[]{:S(2)}) copy-start(bf16[128,3072]{1,0:T(8,128)(2,1)S(1)} %collective-permute-done.5) | copy-start | bytes 2359300
  326.2 15.8 %copy-start.7 = (bf16[3072,128]{1,0:T(8,128)(2,1)}, bf16[3072,128]{1,0:T(8,128)(2,1)S(1)}, u32[]{:S(2)}) copy-start(bf16[3072,128]{1,0:T(8,128)(2,1)S(1)} %collective-permute-done.4) | copy-start | bytes 2359300
  341.3 1.5 copy-start.10
  342.0 1.4 copy-start.20
  344.6 103.8 %collective-permute-start.8 = (f32[3,3072,128]{2,1,0:T(8,128)S(1)}, f32[3,3072,128]{2,1,0:T(8,128)}, u32[]{:S(2)}, u32[]{:S(2)}) collective-permute-start(f32[3,3072,128]{2,1,0:T(8,128)S(1)} %maximum_add_fusion.1), channel_id=1, source_target_pairs={{0,62},{1,63},{2,0},{3,1},{4,2},{5,3},{6,4},{7,5},{8,6},{9,7},{10,... | collective-permute-start | bytes 14155784 | tf_op jit(solution)/shard_map/ppermute | solution.py:16
  448.3 2.1 copy-start.13
  450.4 1.1 copy-start.15
  450.4 1.4 copy-start.17
  451.8 1.1 copy-start.4
  452.9 1.4 copy-start.11
  452.9 1.4 copy-start.21
  452.9 1.4 copy-start.23
  454.3 1.2 copy-start.6
  454.3 1.2 copy-start.19
  (3 other events, 2.7 us)
Sparse Core Ops, SparseCore 0:
  448.5 46.8 reduce-scatter.1
where the time goes:
time: 509 us; the launch traced here: 505 us
  waiting for transfers between devices  452 us (89%)
  matrix products  20.1 us (4%)
  between operations  14.5 us (3%)
  other arithmetic  7.27 us (1%)
  starting transfers between devices  6.72 us (1%)
    ppermute x9, waiting for transfers between devices, from_behind(): return lax.ppermute(value, axis, pairs)  416 us
    reduce_scatter x1, waiting for transfers between devices, shards(): carried = lax.psum_scatter(carried, 'dp', scatter_dimension=1, tiled=True)  35.8 us
  transfers between devices with their start and end apart: 10, of which 8 were waited for; matrix products, arithmetic and copies ran while one was open for 3% of the time, Pallas kernels for 0%

commit v1 on v0

v1 whole, which is shorter than its diff:
```python
import jax
import jax.numpy as jnp
from jax import lax
from jax.sharding import PartitionSpec as P

HOPS = 3
DP = 4


epsilon = 1e-05
grad_scale = 0.0625


def from_behind(value, steps):
    count = lax.axis_size("blk")
    pairs = [(source, (source + steps) % count) for source in range(count)]
    return lax.ppermute(value, "blk", pairs)


def swap(value, bit):
    return lax.ppermute(value, "dp", [(source, source ^ bit) for source in range(DP)])


def wire(value):
    return value.astype(jnp.bfloat16)


def relative_columns(value, place):
    width = value.shape[1] // DP
    blocks = [
        lax.dynamic_slice_in_dim(value, (place ^ k) * width, width, axis=1) for k in range(DP)
    ]
    return jnp.concatenate(blocks, axis=1)


def relative_rows(value, place):
    height = value.shape[0] // DP
    blocks = [
        lax.dynamic_slice_in_dim(value, (place ^ k) * height, height, axis=0) for k in range(DP)
    ]
    return jnp.concatenate(blocks, axis=0)


def shards(tokens, cotangent, norm_gain, gate_weight, up_weight, down_weight):
    contract_rows = (((0,), (0,)), ((), ()))
    contract_cols = (((1,), (1,)), ((), ()))
    place = lax.axis_index("dp")
    model = tokens.shape[1]
    part = model // DP
    units = gate_weight.shape[1]

    quarter = jnp.concatenate(
        [
            lax.dynamic_slice_in_dim(gate_weight, place * part, part, axis=0),
            lax.dynamic_slice_in_dim(up_weight, place * part, part, axis=0),
            jnp.transpose(lax.dynamic_slice_in_dim(down_weight, place * part, part, axis=1)),
        ],
        axis=1,
    )
    first = from_behind(quarter, 1)
    second = from_behind(first, 1)

    def whole(piece):
        half = jnp.concatenate([piece, swap(piece, 2)], axis=0)
        return half, swap(half, 1)

    wide = tokens.astype(jnp.float32)
    inverse = lax.rsqrt(jnp.mean(wide * wide, axis=-1, keepdims=True) + epsilon)
    normed = (wide * inverse * norm_gain).astype(jnp.bfloat16)
    normed_rel = relative_columns(normed, place)
    cot_rel = relative_columns(cotangent, place)

    def order(value):
        cut = [value[:, k * part:(k + 1) * part] for k in range(DP)]
        return (
            jnp.concatenate([cut[0], cut[2]], axis=1),
            jnp.concatenate([cut[1], cut[3]], axis=1),
        )

    normed_near, normed_far = order(normed_rel)
    cot_near, cot_far = order(cot_rel)

    own_rel = relative_rows(
        jnp.concatenate([gate_weight, up_weight, jnp.transpose(down_weight)], axis=1), place
    )
    own = (
        jnp.concatenate([own_rel[:part], own_rel[2 * part:3 * part]], axis=0),
        jnp.concatenate([own_rel[part:2 * part], own_rel[3 * part:]], axis=0),
    )
    held = [own, whole(first), whole(second)]

    hidden_all = []
    delta_all = []
    sums = []
    for near, far in held:
        pre = jnp.dot(normed_near, near[:, :2 * units], preferred_element_type=jnp.float32)
        pre = pre + jnp.dot(normed_far, far[:, :2 * units], preferred_element_type=jnp.float32)
        hidden_grad = jnp.dot(cot_near, near[:, 2 * units:], preferred_element_type=jnp.float32)
        hidden_grad = hidden_grad + jnp.dot(
            cot_far, far[:, 2 * units:], preferred_element_type=jnp.float32
        )
        pre_gate, pre_up = pre[:, :units], pre[:, units:]
        sigmoid_gate = jax.nn.sigmoid(pre_gate)
        active = pre_gate * sigmoid_gate
        hidden = (active * pre_up).astype(jnp.bfloat16)
        gate_delta = (
            hidden_grad * pre_up * sigmoid_gate * (1.0 + pre_gate * (1.0 - sigmoid_gate))
        ).astype(jnp.bfloat16)
        up_delta = (hidden_grad * active).astype(jnp.bfloat16)
        delta = jnp.concatenate([gate_delta, up_delta], axis=1)
        hidden_all.append(hidden)
        delta_all.append(delta)

        def terms(normed_half, cot_half):
            return jnp.concatenate(
                [
                    lax.dot_general(
                        normed_half, delta, contract_rows, preferred_element_type=jnp.float32
                    ),
                    lax.dot_general(
                        cot_half, hidden, contract_rows, preferred_element_type=jnp.float32
                    ),
                ],
                axis=1,
            )

        arrived = swap(wire(terms(normed_far, cot_far)), 1)
        chip = terms(normed_near, cot_near) + arrived
        arrived = swap(wire(chip[part:]), 2)
        sums.append(chip[:part] + arrived)

    hidden = jnp.concatenate(hidden_all, axis=1)
    delta = jnp.concatenate(delta_all, axis=1)

    def outward(value, start, stop):
        halves = []
        for side in range(2):
            weights = jnp.concatenate([pair[side][:, start:stop] for pair in held], axis=1)
            halves.append(
                lax.dot_general(value, weights, contract_cols, preferred_element_type=jnp.float32)
            )
        near, far = halves
        rel = jnp.concatenate(
            [near[:, :part], far[:, :part], near[:, part:], far[:, part:]], axis=1
        )
        return relative_columns(rel, place)

    mlp_total = outward(hidden, 2 * units, 3 * units)
    dnormed = outward(delta, 0, 2 * units)
    block_out = (wide + mlp_total).astype(jnp.bfloat16)
    scaled = wide * inverse
    along = dnormed * norm_gain
    norm_back = inverse * (along - scaled * jnp.mean(along * scaled, axis=-1, keepdims=True))
    input_grad = (cotangent.astype(jnp.float32) + norm_back).astype(jnp.bfloat16)

    carried = sums[2]
    carried = from_behind(wire(carried), -1) + sums[1]
    carried = from_behind(wire(carried), -1) + sums[0]
    carried = carried * grad_scale
    return (
        block_out,
        input_grad,
        carried[:, :units],
        carried[:, units:2 * units],
        jnp.transpose(carried[:, 2 * units:]),
    )


def solution(mesh):
    in_specs = (
        P(("dp", "blk"), None),
        P(("dp", "blk"), None),
        P(),
        P(None, "blk"),
        P(None, "blk"),
        P("blk", None),
    )
    out_specs = (
        P(("dp", "blk"), None),
        P(("dp", "blk"), None),
        P("dp", "blk"),
        P("dp", "blk"),
        P("blk", "dp"),
    )
    return jax.shard_map(shards, mesh=mesh, in_specs=in_specs, out_specs=out_specs, check_vma=False)
```

time: 509 us -> 133 us (0.26)
  waiting for transfers between devices: 452 us -> 80.8 us
  between operations: 14.5 us -> 1.33 us
  matrix products: 20.1 us -> 11.4 us
  local copies, waits for them, and re-layouts: 5.02 us -> 13.1 us
  starting transfers between devices: 6.72 us -> 14.7 us
    ppermute x9 -> x14, waiting for transfers between devices: 416 us -> 80.8 us  [the longest x10 51 us: swap(): lax.ppermute(value, 'dp', [(source, source ^ bit) for source in range(DP)])]
    reduce_scatter x1 -> x0, waiting for transfers between devices: 35.8 us -> none  [shards(): carried = lax.psum_scatter(carried, 'dp', scatter_dimension=1, tiled=True)]
    dot_general x24 -> x28, matrix products: 20.1 us -> 11.4 us  [the longest x4 2.76 us: outward(): lax.dot_general(value, weights, contract_cols, preferred_element_type=jnp...]
    ppermute x9 -> x14, starting transfers between devices: 6.69 us -> 14.7 us  [the longest x4 7.86 us: from_behind(): return lax.ppermute(value, 'blk', pairs)]
  transfers between devices with their start and end apart: 10 -> 14, of which waited for: 8 -> 9; matrix products, arithmetic and copies ran while one was open for 3% -> 18% of each run, Pallas kernels for 0% -> 0%
where the time goes in v1:
time: 133 us; the launch traced here: 131 us
  waiting for transfers between devices  80.8 us (61%)
  starting transfers between devices  14.7 us (11%)
  local copies, waits for them, and re-layouts  13.1 us (10%)
  matrix products  11.4 us (9%)
  other arithmetic  9.58 us (7%)
  between operations  1.33 us (1%)
    ppermute x10, waiting for transfers between devices, swap(): lax.ppermute(value, 'dp', [(source, source ^ bit) for source in range(DP)])  51 us
    ppermute x4, waiting for transfers between devices, from_behind(): return lax.ppermute(value, 'blk', pairs)  29.8 us
    ppermute x4, starting transfers between devices, from_behind(): return lax.ppermute(value, 'blk', pairs)  7.86 us
    unnamed x18, local copies, waits for them, and re-layouts  7.34 us
    ppermute x10, starting transfers between devices, swap(): lax.ppermute(value, 'dp', [(source, source ^ bit) for source in range(DP)])  6.88 us
    dot_general x4, matrix products, outward(): lax.dot_general(value, weights, contract_cols, preferred_element_type=jnp...  2.76 us
  transfers between devices with their start and end apart: 14, of which 9 were waited for; matrix products, arithmetic and copies ran while one was open for 18% of the time, Pallas kernels for 0%

profile of v1, /device:TPU:2, one launch (start us, length us, event | category | flops | bytes accessed | tf_op | source)
XLA Modules:
  0.0 131.0 jit_solution(8262476831136219657)
XLA Ops:
  0.6 1.5 %copy.12 = bf16[3072,128]{0,1:T(8,128)(2,1)S(1)} copy(bf16[3072,128]{1,0:T(8,128)(2,1)} %param.10) | data formatting | bytes 1572864 | tf_op args[4]
  2.4 1.2 dynamic-slice_bitcast_fusion
  3.7 0.9 pad_maximum_fusion.10
  4.6 1.6 %collective-permute-start = (bf16[768,384]{0,1:T(8,128)(2,1)}, bf16[768,384]{0,1:T(8,128)(2,1)}, u32[]{:S(2)}, u32[]{:S(2)}) collective-permute-start(bf16[768,384]{0,1:T(8,128)(2,1)} %pad_maximum_fusion.10), channel_id=1, source_target_pairs={{0,1},{1,2},{2,3},{3,4},{4,5},{5,6},{6,7},{7,8},{8,9},{9,10},{10,1... | collective-permute-start | bytes 1769480 | tf_op jit(solution)/shard_map/ppermute | solution.py:17
  6.1 1.5 %pad_maximum_fusion.2 = bf16[3072,384]{0,1:T(8,128)(2,1)S(1)} fusion(bf16[3072,128]{0,1:T(8,128)(2,1)} %bitcast.17, bf16[3072,128]{0,1:T(8,128)(2,1)S(1)} %copy.12, bf16[3072,128]{0,1:T(8,128)(2,1)} %copy-done.2), kind=kLoop, calls=%fused_computation.23 | loop fusion | flops 7077888 | bytes 4718592 | tf_op jit(solution)/shard_map/concatenate | solution.py:84
  8.2 1.3 copy-done
  10.5 1.2 copy-done.1
  14.5 13.6 %collective-permute-done = bf16[768,384]{0,1:T(8,128)(2,1)} collective-permute-done((bf16[768,384]{0,1:T(8,128)(2,1)}, bf16[768,384]{0,1:T(8,128)(2,1)}, u32[]{:S(2)}, u32[]{:S(2)}) %collective-permute-start) | collective-permute-done | bytes 589856 | tf_op jit(solution)/shard_map/ppermute | solution.py:17
  28.2 1.4 %collective-permute-start.1 = (bf16[768,384]{0,1:T(8,128)(2,1)}, bf16[768,384]{0,1:T(8,128)(2,1)S(1)}, u32[]{:S(2)}, u32[]{:S(2)}) collective-permute-start(bf16[768,384]{0,1:T(8,128)(2,1)} %collective-permute-done), channel_id=1, source_target_pairs={{0,128},{64,192},{128,0},{192,64},{1,129},{65,193},{129,1},{193,65... | collective-permute-start | bytes 1769480 | tf_op jit(solution)/shard_map/ppermute | solution.py:21
  29.6 1.2 constant_dynamic-update-slice_fusion.1
  30.8 12.0 %collective-permute-done.1 = bf16[768,384]{0,1:T(8,128)(2,1)S(1)} collective-permute-done((bf16[768,384]{0,1:T(8,128)(2,1)}, bf16[768,384]{0,1:T(8,128)(2,1)S(1)}, u32[]{:S(2)}, u32[]{:S(2)}) %collective-permute-start.1) | collective-permute-done | bytes 589856 | tf_op jit(solution)/shard_map/ppermute | solution.py:21
  43.7 6.1 %collective-permute-done.3 = bf16[768,384]{0,1:T(8,128)(2,1)S(1)} collective-permute-done((bf16[768,384]{0,1:T(8,128)(2,1)}, bf16[768,384]{0,1:T(8,128)(2,1)S(1)}, u32[]{:S(2)}, u32[]{:S(2)}) %collective-permute-start.3) | collective-permute-done | bytes 589856 | tf_op jit(solution)/shard_map/ppermute | solution.py:17
  50.8 1.5 %collective-permute-start.13 = (bf16[768,384]{0,1:T(8,128)(2,1)S(1)}, bf16[768,384]{0,1:T(8,128)(2,1)S(1)}, u32[]{:S(2)}, u32[]{:S(2)}) collective-permute-start(bf16[768,384]{0,1:T(8,128)(2,1)S(1)} %slice.259), channel_id=1, source_target_pairs={{0,128},{64,192},{128,0},{192,64},{1,129},{65,193},{129,1},{193,65... | collective-permute-start | bytes 1769480 | tf_op jit(solution)/shard_map/ppermute | solution.py:21
  52.3 13.7 %collective-permute-done.4 = bf16[768,384]{0,1:T(8,128)(2,1)S(1)} collective-permute-done((bf16[768,384]{0,1:T(8,128)(2,1)S(1)}, bf16[768,384]{0,1:T(8,128)(2,1)S(1)}, u32[]{:S(2)}, u32[]{:S(2)}) %collective-permute-start.4) | collective-permute-done | bytes 589856 | tf_op jit(solution)/shard_map/ppermute | solution.py:21
  68.8 0.8 collective-permute-start.9
  73.3 0.7 slice-done
  74.0 0.8 fusion.17
  74.9 0.8 fusion.11
  75.9 0.8 slice-done.1
  79.1 1.3 %collective-permute-done.6 = bf16[1536,384]{0,1:T(8,128)(2,1)S(1)} collective-permute-done((bf16[1536,384]{0,1:T(8,128)(2,1)S(1)}, bf16[1536,384]{0,1:T(8,128)(2,1)S(1)}, u32[]{:S(2)}, u32[]{:S(2)}) %collective-permute-start.6) | collective-permute-done | bytes 1179680 | tf_op jit(solution)/shard_map/ppermute | solution.py:21
  80.9 0.7 collective-permute-start.7
  82.6 1.5 %collective-permute-start.10 = (bf16[768,384]{0,1:T(8,128)(2,1)S(1)}, bf16[768,384]{0,1:T(8,128)(2,1)S(1)}, u32[]{:S(2)}, u32[]{:S(2)}) collective-permute-start(bf16[768,384]{0,1:T(8,128)(2,1)S(1)} %slice.260), channel_id=1, source_target_pairs={{0,128},{64,192},{128,0},{192,64},{1,129},{65,193},{129,1},{193,65... | collective-permute-start | bytes 1769480 | tf_op jit(solution)/shard_map/ppermute | solution.py:21
  84.1 13.0 %collective-permute-done.7 = bf16[768,384]{0,1:T(8,128)(2,1)S(1)} collective-permute-done((bf16[768,384]{0,1:T(8,128)(2,1)S(1)}, bf16[768,384]{0,1:T(8,128)(2,1)S(1)}, u32[]{:S(2)}, u32[]{:S(2)}) %collective-permute-start.7) | collective-permute-done | bytes 589856 | tf_op jit(solution)/shard_map/ppermute | solution.py:21
  97.4 0.7 fusion.4
  98.1 10.9 %collective-permute-done.10 = bf16[768,384]{0,1:T(8,128)(2,1)S(1)} collective-permute-done((bf16[768,384]{0,1:T(8,128)(2,1)S(1)}, bf16[768,384]{0,1:T(8,128)(2,1)S(1)}, u32[]{:S(2)}, u32[]{:S(2)}) %collective-permute-start.10) | collective-permute-done | bytes 589856 | tf_op jit(solution)/shard_map/ppermute | solution.py:21
  109.0 2.2 %collective-permute-done.8 = bf16[768,384]{0,1:T(8,128)(2,1)S(1)} collective-permute-done((bf16[768,384]{0,1:T(8,128)(2,1)S(1)}, bf16[768,384]{0,1:T(8,128)(2,1)S(1)}, u32[]{:S(2)}, u32[]{:S(2)}) %collective-permute-start.8) | collective-permute-done | bytes 589856 | tf_op jit(solution)/shard_map/ppermute | solution.py:17
  111.4 6.2 %collective-permute-start.11 = (bf16[768,384]{0,1:T(8,128)(2,1)S(1)}, bf16[768,384]{0,1:T(8,128)(2,1)S(1)}, u32[]{:S(2)}, u32[]{:S(2)}) collective-permute-start(bf16[768,384]{0,1:T(8,128)(2,1)S(1)} %fusion.26), channel_id=1, source_target_pairs={{0,63},{1,0},{2,1},{3,2},{4,3},{5,4},{6,5},{7,6},{8,7},{9,8},{10,9... | collective-permute-start | bytes 1769480 | tf_op jit(solution)/shard_map/ppermute | solution.py:17
  117.6 2.6 %fusion.8 = (bf16[256,3072]{1,0:T(8,128)(2,1)}, bf16[256,3072]{1,0:T(8,128)(2,1)}) fusion(bf16[256,3072]{1,0:T(8,128)(2,1)S(1)} %copy-done, bf16[256,3072]{1,0:T(8,128)(2,1)S(1)} %copy-done.1, f32[256,768]{1,0:T(8,128)S(1)} %get-tuple-element.23, f32[256,768]{1,0:T(8,128)S(1)} %get-tuple-element.24, f32[256,768]{1,0:T(8,128)S(1)} %get-tuple-element.25, ...), kind=kLoop, calls=%fused_computation.11 | loop fusion | flops 13369344 | bytes 12597248 | tf_op jit(solution)/shard_map/convert_element_type | solution.py:154
  120.2 7.9 %collective-permute-done.11 = bf16[768,384]{0,1:T(8,128)(2,1)S(1)} collective-permute-done((bf16[768,384]{0,1:T(8,128)(2,1)S(1)}, bf16[768,384]{0,1:T(8,128)(2,1)S(1)}, u32[]{:S(2)}, u32[]{:S(2)}) %collective-permute-start.11) | collective-permute-done | bytes 589856 | tf_op jit(solution)/shard_map/ppermute | solution.py:17
  128.3 0.8 slice_bitcast_fusion
  129.2 0.9 copy.15
  130.1 0.9 copy.16
  (98 shorter events, 17.4 us)
Async XLA Ops:
  0.6 1.5 %copy-start.4 = (bf16[3072,128]{1,0:T(8,128)(2,1)S(1)}, bf16[3072,128]{1,0:T(8,128)(2,1)}, u32[]{:S(2)}) copy-start(bf16[3072,128]{1,0:T(8,128)(2,1)} %param.9) | copy-start | bytes 2359300
  2.4 3.7 %copy-start.2 = (bf16[3072,128]{0,1:T(8,128)(2,1)}, bf16[3072,128]{0,1:T(8,128)(2,1)S(1)}, u32[]{:S(2)}) copy-start(bf16[3072,128]{0,1:T(8,128)(2,1)S(1)} %copy.11) | copy-start | bytes 2359300
  4.6 23.6 %collective-permute-start = (bf16[768,384]{0,1:T(8,128)(2,1)}, bf16[768,384]{0,1:T(8,128)(2,1)}, u32[]{:S(2)}, u32[]{:S(2)}) collective-permute-start(bf16[768,384]{0,1:T(8,128)(2,1)} %pad_maximum_fusion.10), channel_id=1, source_target_pairs={{0,1},{1,2},{2,3},{3,4},{4,5},{5,6},{6,7},{7,8},{8,9},{9,10},{10,1... | collective-permute-start | bytes 1769480 | tf_op jit(solution)/shard_map/ppermute | solution.py:17
  8.0 1.4 %copy-start = (bf16[256,3072]{1,0:T(8,128)(2,1)S(1)}, bf16[256,3072]{1,0:T(8,128)(2,1)}, u32[]{:S(2)}) copy-start(bf16[256,3072]{1,0:T(8,128)(2,1)} %param.6) | copy-start | bytes 4718596
  8.1 1.7 %copy-start.5 = (f32[3072]{0:T(1024)S(1)}, f32[3072]{0:T(1024)}, u32[]{:S(2)}) copy-start(f32[3072]{0:T(1024)} %param.8) | copy-start | bytes 36868
  10.4 1.4 %copy-start.1 = (bf16[256,3072]{1,0:T(8,128)(2,1)S(1)}, bf16[256,3072]{1,0:T(8,128)(2,1)}, u32[]{:S(2)}) copy-start(bf16[256,3072]{1,0:T(8,128)(2,1)} %param.7) | copy-start | bytes 4718596
  14.4 35.9 %collective-permute-start.12 = (bf16[1536,384]{0,1:T(8,128)(2,1)S(1)}, bf16[1536,384]{0,1:T(8,128)(2,1)S(1)}, u32[]{:S(2)}, u32[]{:S(2)}) collective-permute-start(bf16[1536,384]{0,1:T(8,128)(2,1)S(1)} %pad_maximum_fusion.5), channel_id=1, source_target_pairs={{0,64},{64,0},{128,192},{192,128},{1,65},{65,1},{129,193},{193,129... | collective-permute-start | bytes 3538952 | tf_op jit(solution)/shard_map/ppermute | solution.py:21
  28.2 14.6 %collective-permute-start.1 = (bf16[768,384]{0,1:T(8,128)(2,1)}, bf16[768,384]{0,1:T(8,128)(2,1)S(1)}, u32[]{:S(2)}, u32[]{:S(2)}) collective-permute-start(bf16[768,384]{0,1:T(8,128)(2,1)} %collective-permute-done), channel_id=1, source_target_pairs={{0,128},{64,192},{128,0},{192,64},{1,129},{65,193},{129,1},{193,65... | collective-permute-start | bytes 1769480 | tf_op jit(solution)/shard_map/ppermute | solution.py:21
  29.6 20.2 %collective-permute-start.3 = (bf16[768,384]{0,1:T(8,128)(2,1)}, bf16[768,384]{0,1:T(8,128)(2,1)S(1)}, u32[]{:S(2)}, u32[]{:S(2)}) collective-permute-start(bf16[768,384]{0,1:T(8,128)(2,1)} %collective-permute-done), channel_id=1, source_target_pairs={{0,1},{1,2},{2,3},{3,4},{4,5},{5,6},{6,7},{7,8},{8,9},{9,10},{10,1... | collective-permute-start | bytes 1769480 | tf_op jit(solution)/shard_map/ppermute | solution.py:17
  42.8 23.5 %collective-permute-start.2 = (bf16[1536,384]{0,1:T(8,128)(2,1)S(1)}, bf16[1536,384]{0,1:T(8,128)(2,1)S(1)}, u32[]{:S(2)}, u32[]{:S(2)}) collective-permute-start(bf16[1536,384]{0,1:T(8,128)(2,1)S(1)} %constant_dynamic-update-slice_fusion), channel_id=1, source_target_pairs={{0,64},{64,0},{128,192},{192,128},{1,65},{65,1},{129,193},{193,129... | collective-permute-start | bytes 3538952 | tf_op jit(solution)/shard_map/ppermute | solution.py:21
  49.8 16.3 %collective-permute-start.4 = (bf16[768,384]{0,1:T(8,128)(2,1)S(1)}, bf16[768,384]{0,1:T(8,128)(2,1)S(1)}, u32[]{:S(2)}, u32[]{:S(2)}) collective-permute-start(bf16[768,384]{0,1:T(8,128)(2,1)S(1)} %collective-permute-done.3), channel_id=1, source_target_pairs={{0,128},{64,192},{128,0},{192,64},{1,129},{65,193},{129,1},{193,65... | collective-permute-start | bytes 1769480 | tf_op jit(solution)/shard_map/ppermute | solution.py:21
  50.8 69.4 %collective-permute-start.13 = (bf16[768,384]{0,1:T(8,128)(2,1)S(1)}, bf16[768,384]{0,1:T(8,128)(2,1)S(1)}, u32[]{:S(2)}, u32[]{:S(2)}) collective-permute-start(bf16[768,384]{0,1:T(8,128)(2,1)S(1)} %slice.259), channel_id=1, source_target_pairs={{0,128},{64,192},{128,0},{192,64},{1,129},{65,193},{129,1},{193,65... | collective-permute-start | bytes 1769480 | tf_op jit(solution)/shard_map/ppermute | solution.py:21
  66.1 4.1 %collective-permute-start.5 = (bf16[1536,384]{0,1:T(8,128)(2,1)S(1)}, bf16[1536,384]{0,1:T(8,128)(2,1)S(1)}, u32[]{:S(2)}, u32[]{:S(2)}) collective-permute-start(bf16[1536,384]{0,1:T(8,128)(2,1)S(1)} %constant_dynamic-update-slice_fusion.2), channel_id=1, source_target_pairs={{0,64},{64,0},{128,192},{192,128},{1,65},{65,1},{129,193},{193,129... | collective-permute-start | bytes 3538952 | tf_op jit(solution)/shard_map/ppermute | solution.py:21
  66.3 3.3 %copy-start.3 = (bf16[1536,384]{0,1:T(8,128)(2,1)}, bf16[1536,384]{0,1:T(8,128)(2,1)S(1)}, u32[]{:S(2)}) copy-start(bf16[1536,384]{0,1:T(8,128)(2,1)S(1)} %collective-permute-done.2) | copy-start | bytes 3538948
  68.8 13.4 %collective-permute-start.9 = (bf16[1536,384]{0,1:T(8,128)(2,1)S(1)}, bf16[1536,384]{0,1:T(8,128)(2,1)S(1)}, u32[]{:S(2)}, u32[]{:S(2)}) collective-permute-start(bf16[1536,384]{0,1:T(8,128)(2,1)S(1)} %pad_maximum_fusion.4), channel_id=1, source_target_pairs={{0,64},{64,0},{128,192},{192,128},{1,65},{65,1},{129,193},{193,129... | collective-permute-start | bytes 3538952 | tf_op jit(solution)/shard_map/ppermute | solution.py:21
  72.9 1.1 slice-start
  75.7 1.0 slice-start.1
  77.5 2.9 %collective-permute-start.6 = (bf16[1536,384]{0,1:T(8,128)(2,1)S(1)}, bf16[1536,384]{0,1:T(8,128)(2,1)S(1)}, u32[]{:S(2)}, u32[]{:S(2)}) collective-permute-start(bf16[1536,384]{0,1:T(8,128)(2,1)S(1)} %pad_maximum_fusion.3), channel_id=1, source_target_pairs={{0,64},{64,0},{128,192},{192,128},{1,65},{65,1},{129,193},{193,129... | collective-permute-start | bytes 3538952 | tf_op jit(solution)/shard_map/ppermute | solution.py:21
  80.9 16.3 %collective-permute-start.7 = (bf16[768,384]{0,1:T(8,128)(2,1)S(1)}, bf16[768,384]{0,1:T(8,128)(2,1)S(1)}, u32[]{:S(2)}, u32[]{:S(2)}) collective-permute-start(bf16[768,384]{0,1:T(8,128)(2,1)S(1)} %slice.261), channel_id=1, source_target_pairs={{0,128},{64,192},{128,0},{192,64},{1,129},{65,193},{129,1},{193,65... | collective-permute-start | bytes 1769480 | tf_op jit(solution)/shard_map/ppermute | solution.py:21
  82.6 26.4 %collective-permute-start.10 = (bf16[768,384]{0,1:T(8,128)(2,1)S(1)}, bf16[768,384]{0,1:T(8,128)(2,1)S(1)}, u32[]{:S(2)}, u32[]{:S(2)}) collective-permute-start(bf16[768,384]{0,1:T(8,128)(2,1)S(1)} %slice.260), channel_id=1, source_target_pairs={{0,128},{64,192},{128,0},{192,64},{1,129},{65,193},{129,1},{193,65... | collective-permute-start | bytes 1769480 | tf_op jit(solution)/shard_map/ppermute | solution.py:21
  97.3 13.8 %collective-permute-start.8 = (bf16[768,384]{0,1:T(8,128)(2,1)S(1)}, bf16[768,384]{0,1:T(8,128)(2,1)S(1)}, u32[]{:S(2)}, u32[]{:S(2)}) collective-permute-start(bf16[768,384]{0,1:T(8,128)(2,1)S(1)} %fusion.27), channel_id=1, source_target_pairs={{0,63},{1,0},{2,1},{3,2},{4,3},{5,4},{6,5},{7,6},{8,7},{9,8},{10,9... | collective-permute-start | bytes 1769480 | tf_op jit(solution)/shard_map/ppermute | solution.py:17
  111.4 16.8 %collective-permute-start.11 = (bf16[768,384]{0,1:T(8,128)(2,1)S(1)}, bf16[768,384]{0,1:T(8,128)(2,1)S(1)}, u32[]{:S(2)}, u32[]{:S(2)}) collective-permute-start(bf16[768,384]{0,1:T(8,128)(2,1)S(1)} %fusion.26), channel_id=1, source_target_pairs={{0,63},{1,0},{2,1},{3,2},{4,3},{5,4},{6,5},{7,6},{8,7},{9,8},{10,9... | collective-permute-start | bytes 1769480 | tf_op jit(solution)/shard_map/ppermute | solution.py:17

commit v2 on v0

v2 whole, which is shorter than its diff:
```python
import functools

import jax
import jax.numpy as jnp
from jax import lax
from jax.experimental import pallas as pl
from jax.experimental.pallas import tpu as pltpu
from jax.sharding import PartitionSpec as P

DP = 4
RING = 4
TIE_LIMIT = 1024 * 1024
VMEM_LIMIT = 12 * 1024 * 1024


epsilon = 1e-05
grad_scale = 0.0625

BOTH = ("dp", "blk")
NN = (((1,), (0,)), ((), ()))
FLAG = ((8, 128), jnp.float32)
NT = (((1,), (1,)), ((), ()))
TN = (((0,), (0,)), ((), ()))
STRIP = 16


def mul(left, right, dims=NN):
    return lax.dot_general(left, right, dims, preferred_element_type=jnp.float32)


def move(value, target):
    count = lax.axis_size("blk")
    pairs = []
    for place in range(DP):
        for block in range(count):
            to_place, to_block = target(place, block)
            pairs.append((place * count + block, to_place * count + to_block % count))
    return lax.ppermute(value, BOTH, pairs)


def swap(value, bit):
    return lax.ppermute(value, "dp", [(source, source ^ bit) for source in range(DP)])


def turn(block, step):
    return block // RING * RING + (block + step) % RING


def half_of(count):
    return count // 2


def forward(value):
    def target(place, block):
        half = half_of(lax.axis_size("blk"))
        return place ^ (2 if block % half == half - 1 else 0), block + 1

    return move(value, target)


def backward(value):
    def target(place, block):
        half = half_of(lax.axis_size("blk"))
        return place ^ (2 if block % half == 0 else 0), block - 1

    return move(value, target)


def back_two(value):
    def target(place, block):
        half = half_of(lax.axis_size("blk"))
        return place ^ (2 if block % half < 2 else 0), block - 2

    return move(value, target)


def around_first(value):
    return move(value, lambda place, block: (place, turn(block, -1)))


def around_second(value):
    def target(place, block):
        half = half_of(lax.axis_size("blk"))
        source = turn(block, 1)
        return place ^ (2 if source % half >= half - 2 else 0), source + 2

    return move(value, target)


def call(kernel, operands, shapes, micros, far=(), tokens=(), scalars=(), scratch=(), direct=False, flag=False):
    whole = pl.BlockSpec(memory_space=pltpu.VMEM)
    anywhere = pl.BlockSpec(memory_space=pl.ANY)
    hbm = pl.BlockSpec(memory_space=pltpu.HBM)
    in_specs = [pl.BlockSpec(memory_space=pltpu.SMEM)] * len(scalars) + [whole] * len(operands)
    return pl.pallas_call(
        kernel,
        out_shape=[jax.ShapeDtypeStruct(s, d) for s, d in list(shapes) + [FLAG] * flag],
        in_specs=in_specs + [hbm] * len(far) + [anywhere] * len(tokens),
        out_specs=[hbm if direct else whole] * len(shapes) + [whole] * flag,
        scratch_shapes=list(scratch),
        compiler_params=pltpu.CompilerParams(vmem_limit_bytes=VMEM_LIMIT),
        cost_estimate=pl.CostEstimate(
            flops=int(micros * 1000000000), bytes_accessed=0, transcendentals=0
        ),
    )(*[v[None] for v in scalars], *operands, *far, *tokens)


def after(value, *tokens):
    anywhere = pl.BlockSpec(memory_space=pl.ANY)
    return pl.pallas_call(
        lambda *refs: None,
        out_shape=jax.ShapeDtypeStruct(value.shape, value.dtype),
        in_specs=[anywhere] * (1 + len(tokens)),
        out_specs=anywhere,
        input_output_aliases={0: 0},
        compiler_params=pltpu.CompilerParams(vmem_limit_bytes=TIE_LIMIT),
        cost_estimate=pl.CostEstimate(flops=0, bytes_accessed=0, transcendentals=0),
    )(value, *tokens)


def fetch(sources, targets, sems):
    copies = [
        pltpu.make_async_copy(source, target, sems.at[i])
        for i, (source, target) in enumerate(zip(sources, targets))
    ]
    for copy in copies:
        copy.start()
    return copies


def middle(pre_gate, pre_up, hidden_grad):
    sigmoid_gate = jax.nn.sigmoid(pre_gate)
    active = pre_gate * sigmoid_gate
    hidden = (active * pre_up).astype(jnp.bfloat16)
    gate_delta = (
        hidden_grad * pre_up * sigmoid_gate * (1.0 + pre_gate * (1.0 - sigmoid_gate))
    ).astype(jnp.bfloat16)
    up_delta = (hidden_grad * active).astype(jnp.bfloat16)
    return hidden, jnp.concatenate([gate_delta, up_delta], axis=1)


def columns(place, part, k, start, size):
    return pl.ds(pl.multiple_of((place ^ k) * part + start, 128), size)


def write_terms(place, part, units, hidden, delta, normed, cot, send, keep):
    half = part // 2
    for k in (1, 3, 0, 2):
        for side in range(2):
            at = columns(place, part, k, side * half, half)
            if k % 2:
                out = send[k // 2 * 2 + side]
                into = slice(0, half)
            else:
                out = keep
                into = slice(k // 2 * part + side * half, k // 2 * part + (side + 1) * half)
            out[:2 * units, into] = mul(delta, normed[:, at], TN).astype(out.dtype)
            out[2 * units:, into] = mul(hidden, cot[:, at], TN).astype(out.dtype)


def pack_kernel(part, units, place_ref, place_1, place_2, gate, up, down, low, high, other, gates, ups, downs, sems):
    place = place_ref[0]
    half = part // 2
    sources, targets = [], []
    for i, k in enumerate((0, 2)):
        at = columns(place, part, k, 0, part)
        sources += [gate.at[at, :], up.at[at, :], down.at[:, at]]
        targets += [gates.at[i], ups.at[i], downs.at[i]]
    copies = fetch(sources, targets, sems)
    for copy in copies[:3]:
        copy.wait()
    for out, start in ((low, 0), (high, half)):
        out[:, :units] = gates[0, start:start + half, :]
        out[:, units:2 * units] = ups[0, start:start + half, :]
        out[:, 2 * units:] = jnp.transpose(downs[0, :, start:start + half])
    for copy in copies[3:]:
        copy.wait()
    other[:, :units] = gates[1]
    other[:, units:2 * units] = ups[1]
    other[:, 2 * units:] = jnp.transpose(downs[1])


def own_kernel(gain, tokens_far, cot_far, gate_far, up_far, down_far, *rest):
    cot, normed, inverse_ref, hidden_ref, delta_ref, tokens, gate, up, down, sems = rest[-10:]
    copies = fetch(
        (tokens_far, cot_far, gate_far, up_far, down_far), (tokens, cot, gate, up, down), sems
    )
    copies[0].wait()

    def strip(i, carry):
        rows = pl.ds(pl.multiple_of(i * STRIP, STRIP), STRIP)
        wide = tokens[rows, :].astype(jnp.float32)
        inverse = lax.rsqrt(jnp.mean(wide * wide, axis=-1, keepdims=True) + epsilon)
        inverse_ref[rows, :] = inverse
        normed[rows, :] = (wide * inverse * gain[...]).astype(jnp.bfloat16)
        return carry

    lax.fori_loop(0, tokens.shape[0] // STRIP, strip, 0)
    for copy in copies[1:]:
        copy.wait()
    hidden, delta = middle(
        mul(normed[...], gate[...]), mul(normed[...], up[...]), mul(cot[...], down[...], NT)
    )
    hidden_ref[...] = hidden
    delta_ref[...] = delta


def terms_kernel(part, units, place_ref, normed, cot, hidden, delta, *rest):
    write_terms(
        place_ref[0], part, units, hidden[...], delta[...], normed, cot, rest[-5:-1], rest[-1]
    )


def shard_kernel(part, units, layout, place_ref, normed, cot, *rest):
    pieces = rest[:len(layout)]
    hidden_ref, delta_ref = rest[-7:-5]
    send, keep = rest[-5:-1], rest[-1]
    place = place_ref[0]
    pre = None
    grad = None
    for (k, start, size), piece in zip(layout, pieces):
        at = columns(place, part, k, start, size)
        pre_here = mul(normed[:, at], piece[:, :2 * units])
        grad_here = mul(cot[:, at], piece[:, 2 * units:])
        pre = pre_here if pre is None else pre + pre_here
        grad = grad_here if grad is None else grad + grad_here
    hidden, delta = middle(pre[:, :units], pre[:, units:], grad)
    hidden_ref[...] = hidden
    delta_ref[...] = delta
    write_terms(place, part, units, hidden, delta, normed, cot, send, keep)


def summed(part, keep, arrived):
    half = part // 2
    return [keep[:, i * half:(i + 1) * half] + arrived[i][...].astype(jnp.float32) for i in range(DP)]


def add_kernel(part, keep, *rest):
    half = part // 2
    total = summed(part, keep, rest[:DP])
    out, mine = rest[-2:]
    mine[:, :half] = total[0]
    mine[:, half:] = total[1]
    out[:, :half] = total[2].astype(jnp.bfloat16)
    out[:, half:] = total[3].astype(jnp.bfloat16)


def last_add_kernel(part, keep, mine_1, here_1, *rest):
    half = part // 2
    total = summed(part, keep, rest[:DP])
    low, high, mine, near = rest[-4:]
    mine[:, :half] = total[0]
    mine[:, half:] = total[1]
    low[...] = total[2].astype(jnp.bfloat16)
    high[...] = total[3].astype(jnp.bfloat16)
    near[...] = (mine_1[...] + here_1[...].astype(jnp.float32)).astype(jnp.bfloat16)


def hop_kernel(start, mine, arrived, *rest):
    size = arrived.shape[1]
    total = mine[:, start:start + size] + arrived[...].astype(jnp.float32)
    if start == 0:
        later, out, later_out = rest[0], rest[-2], rest[-1]
        later_out[...] = later[...]
    else:
        out = rest[-1]
    out[...] = total.astype(jnp.bfloat16)


def final_kernel(units, mine, here, near, low, high, gate, up, down, keep_g, keep_u, keep_d, sems):
    half = low.shape[1]
    for start, last in ((0, low), (half, high)):
        at = slice(start, start + half)
        total = mine[:, at] + here[:, at].astype(jnp.float32) + near[:, at].astype(jnp.float32)
        total = (total + last[...].astype(jnp.float32)) * grad_scale
        keep_g[at, :] = jnp.transpose(total[:units])
        keep_u[at, :] = jnp.transpose(total[units:2 * units])
        keep_d[:, at] = total[2 * units:]
    for copy in fetch((keep_g, keep_u, keep_d), (gate, up, down), sems):
        copy.wait()


def strips(rows, kept, far, sems, body):
    group = rows // DP
    copies = []
    for g in range(DP):
        def strip(i, carry):
            body(pl.ds(pl.multiple_of(g * group + i * STRIP, STRIP), STRIP))
            return carry

        lax.fori_loop(0, group // STRIP, strip, 0)
        here = pl.ds(g * group, group)
        copies.append(pltpu.make_async_copy(kept.at[here, :], far.at[here, :], sems.at[g]))
        copies[-1].start()
    for copy in copies:
        copy.wait()


def forward_out_kernel(part, units, layouts, place_1, place_2, hidden_0, hidden_1, hidden_2, *rest):
    count = len(layouts[0]) + len(layouts[1])
    pieces, rest = rest[:count], rest[count:]
    tokens_far, down_far = rest[:2]
    block_out, flag, tokens, down, mlp, kept, in_sems, out_sems = rest[-8:]
    flag[...] = jnp.zeros_like(flag)
    copies = fetch((down_far, tokens_far), (down, tokens), in_sems)
    copies[0].wait()
    for j in range(DP):
        at = pl.ds(j * part, part)
        mlp[:, at] = mul(hidden_0[...], down[:, at])
    used = 0
    for place_ref, layout, hidden in ((place_1, layouts[0], hidden_1), (place_2, layouts[1], hidden_2)):
        place = place_ref[0]
        for k, start, size in layout:
            at = columns(place, part, k, start, size)
            mlp[:, at] += mul(hidden[...], pieces[used][:, 2 * units:], NT)
            used += 1
    copies[1].wait()

    def body(rows):
        kept[rows, :] = (tokens[rows, :].astype(jnp.float32) + mlp[rows, :]).astype(jnp.bfloat16)

    strips(tokens.shape[0], kept, block_out, out_sems, body)


def backward_out_kernel(part, units, layouts, place_1, place_2, cot, gain, inverse_ref, delta_0, delta_1, delta_2, *rest):
    count = len(layouts[0]) + len(layouts[1])
    pieces, rest = rest[:count], rest[count:]
    tokens_far, gate_far, up_far, input_grad, flag, tokens, gate, up, dnormed, kept, in_sems, out_sems = rest
    flag[...] = jnp.zeros_like(flag)
    copies = fetch((gate_far, up_far, tokens_far), (gate, up, tokens), in_sems)
    for copy in copies[:2]:
        copy.wait()
    for j in range(DP):
        at = pl.ds(j * part, part)
        dnormed[:, at] = mul(delta_0[:, :units], gate[at, :], NT) + mul(
            delta_0[:, units:], up[at, :], NT
        )
    used = 0
    for place_ref, layout, delta in ((place_1, layouts[0], delta_1), (place_2, layouts[1], delta_2)):
        place = place_ref[0]
        for k, start, size in layout:
            at = columns(place, part, k, start, size)
            dnormed[:, at] += mul(delta[...], pieces[used][:, :2 * units], NT)
            used += 1
    copies[2].wait()

    def body(rows):
        wide = tokens[rows, :].astype(jnp.float32)
        inverse = inverse_ref[rows, :]
        scaled = wide * inverse
        along = dnormed[rows, :] * gain[...]
        norm_back = inverse * (along - scaled * jnp.mean(along * scaled, axis=-1, keepdims=True))
        kept[rows, :] = (cot[rows, :].astype(jnp.float32) + norm_back).astype(jnp.bfloat16)

    strips(tokens.shape[0], kept, input_grad, out_sems, body)


def shards(tokens, cotangent, norm_gain, gate_weight, up_weight, down_weight):
    place = lax.axis_index("dp")
    block = lax.axis_index("blk")
    span = half_of(lax.axis_size("blk"))
    rows, model = tokens.shape
    part = model // DP
    half = part // 2
    units = gate_weight.shape[1]
    width = 3 * units
    bf16, f32 = jnp.bfloat16, jnp.float32
    place_1 = place ^ jnp.where(block % span < 1, 2, 0)
    place_2 = place ^ jnp.where(block % span < 2, 2, 0)
    gate_weight, up_weight, down_weight, tokens = (
        pltpu.with_memory_space_constraint(v, pltpu.HBM)
        for v in (gate_weight, up_weight, down_weight, tokens)
    )
    weights = [gate_weight, up_weight, down_weight]
    gain = norm_gain[None, :]
    dma = pltpu.SemaphoreType.DMA

    low, high, other = call(
        functools.partial(pack_kernel, part, units), [],
        [((half, width), bf16)] * 2 + [((part, width), bf16)], 2, far=weights,
        scalars=(place, place_1, place_2),
        scratch=[pltpu.VMEM((2, part, units), bf16)] * 2
        + [pltpu.VMEM((2, units, part), bf16), dma((6,))],
    )
    one_a = forward(low)
    one_b = forward(high)
    two_z = around_first(other)

    acts = [((rows, units), bf16), ((rows, 2 * units), bf16)]
    terms = [((width, half), bf16)] * 4 + [((width, 2 * part), f32)]

    cot, normed, inverse, hidden_0, delta_0 = call(
        own_kernel, [gain], [((rows, model), bf16)] * 2 + [((rows, 1), f32)] + acts, 4,
        far=[tokens, cotangent] + weights, tokens=(other,),
        scratch=[pltpu.VMEM((rows, model), bf16)] + [pltpu.VMEM((model, units), bf16)] * 2
        + [pltpu.VMEM((units, model), bf16), dma((5,))],
    )

    one_a = after(one_a, hidden_0)
    *send, keep = call(
        functools.partial(terms_kernel, part, units), [normed, cot, hidden_0, delta_0], terms, 3,
        scalars=(place,), tokens=(one_a,),
    )
    one_xa = swap(one_a, 2)
    two_a = forward(one_a)
    one_b = after(one_b, keep, one_xa)
    one_xb = swap(one_b, 2)
    two_b = forward(one_b)
    two_z = around_second(two_z)
    ones = [one_a, one_b, one_xa, one_xb]
    ones = ones + [swap(v, 1) for v in ones]
    layout_1 = [(k, start, half) for k in (0, 2, 1, 3) for start in (0, half)]
    twos = [two_a, two_b, two_z]
    twos = twos + [swap(v, 1) for v in twos]
    layout_2 = [(0, 0, half), (0, half, half), (2, 0, part), (1, 0, half), (1, half, half), (3, 0, part)]

    def add(keep, send, tokens=()):
        return call(
            functools.partial(add_kernel, part), [keep] + [swap(v, 1) for v in send],
            [((width, part), bf16), ((width, part), f32)], 1, tokens=tokens,
        )

    out_0, mine_0 = add(keep, send, (one_xb, two_a))
    here_0 = swap(out_0, 2)

    hidden_1, delta_1, *send, keep = call(
        functools.partial(shard_kernel, part, units, layout_1), [normed, cot] + ones,
        acts + terms, 4, scalars=(place_1,), tokens=(out_0, two_b),
    )
    out_1, mine_1 = add(keep, send, (here_0,))
    here_1 = swap(out_1, 2)

    hidden_2, delta_2, *send, keep = call(
        functools.partial(shard_kernel, part, units, layout_2), [normed, cot] + twos,
        acts + terms, 4, scalars=(place_2,), tokens=(hidden_1,),
    )
    input_grad, flag_backward = call(
        functools.partial(backward_out_kernel, part, units, (layout_1, layout_2)),
        [cot, gain, inverse, delta_0, delta_1, delta_2] + ones + twos,
        [((rows, model), bf16)], 5,
        far=[tokens, gate_weight, up_weight], scalars=(place_1, place_2), direct=True, flag=True,
        scratch=[
            pltpu.VMEM((rows, model), bf16), pltpu.VMEM((model, units), bf16),
            pltpu.VMEM((model, units), bf16), pltpu.VMEM((rows, model), f32),
            pltpu.VMEM((rows, model), bf16), dma((3,)), dma((DP,)),
        ],
    )

    low_2, high_2, mine_2, near = call(
        functools.partial(last_add_kernel, part),
        [keep, mine_1, here_1] + [swap(v, 1) for v in send],
        [((width, half), bf16)] * 2 + [((width, part), f32), ((width, part), bf16)], 1,
        tokens=(flag_backward,),
    )
    near = backward(near)

    block_out, flag_forward = call(
        functools.partial(forward_out_kernel, part, units, (layout_1, layout_2)),
        [hidden_0, hidden_1, hidden_2] + ones + twos, [((rows, model), bf16)], 4,
        far=[tokens, down_weight], tokens=(low_2,), scalars=(place_1, place_2), direct=True, flag=True,
        scratch=[
            pltpu.VMEM((rows, model), bf16), pltpu.VMEM((units, model), bf16),
            pltpu.VMEM((rows, model), f32), pltpu.VMEM((rows, model), bf16), dma((2,)), dma((DP,)),
        ],
    )
    sum_low, high_2 = call(
        functools.partial(hop_kernel, 0), [mine_2, swap(low_2, 2), high_2],
        [((width, half), bf16)] * 2, 0.5, tokens=(flag_forward,),
    )
    sum_low = back_two(sum_low)
    sum_high, = call(
        functools.partial(hop_kernel, half), [mine_2, swap(high_2, 2)],
        [((width, half), bf16)], 0.5, tokens=(near,),
    )
    sum_high = back_two(sum_high)

    gate_grad, up_grad, down_grad = call(
        functools.partial(final_kernel, units), [mine_0, here_0, near, sum_low, sum_high],
        [((part, units), f32)] * 2 + [((units, part), f32)], 2, direct=True,
        scratch=[pltpu.VMEM((part, units), f32)] * 2 + [pltpu.VMEM((units, part), f32), dma((3,))],
    )
    return block_out, input_grad, gate_grad, up_grad, down_grad


def solution(mesh):
    in_specs = (
        P(("dp", "blk"), None),
        P(("dp", "blk"), None),
        P(),
        P(None, "blk"),
        P(None, "blk"),
        P("blk", None),
    )
    out_specs = (
        P(("dp", "blk"), None),
        P(("dp", "blk"), None),
        P("dp", "blk"),
        P("dp", "blk"),
        P("blk", "dp"),
    )
    return jax.shard_map(shards, mesh=mesh, in_specs=in_specs, out_specs=out_specs, check_vma=False)
```

time: 509 us -> 117 us (0.23)
  waiting for transfers between devices: 452 us -> 60.7 us
  Pallas kernels: 0 us -> 26.5 us
  starting transfers between devices: 6.72 us -> 28.2 us
  matrix products: 20.1 us -> 0 us
  between operations: 14.5 us -> 1.04 us
  other arithmetic: 7.27 us -> 0 us
    ppermute x9 -> x34, waiting for transfers between devices: 416 us -> 60.7 us  [the longest x9 43.6 us: move(): return lax.ppermute(value, BOTH, pairs)]
    reduce_scatter x1 -> x0, waiting for transfers between devices: 35.8 us -> none  [shards(): carried = lax.psum_scatter(carried, 'dp', scatter_dimension=1, tiled=True)]
    pallas_call x0 -> x15, Pallas kernels: none -> 26.5 us  [the longest x13 26.5 us: call(): pl.pallas_call(kernel, out_shape=[jax.ShapeDtypeStruct(s, d) for s, d in...]
    ppermute x9 -> x34, starting transfers between devices: 6.69 us -> 28.2 us  [the longest x25 16.9 us: swap(): lax.ppermute(value, 'dp', [(source, source ^ bit) for source in range(DP)])]
    dot_general x24 -> x0, matrix products: 20.1 us -> none  [the longest x3 3.88 us: shards(): lax.dot_general(both_deltas, both_parts, contract_cols, preferred_element...]
  transfers between devices with their start and end apart: 10 -> 34, of which waited for: 8 -> 13; matrix products, arithmetic and copies ran while one was open for 3% -> 0% of each run, Pallas kernels for 0% -> 20%
where the time goes in v2:
time: 117 us; the launch traced here: 116 us
  waiting for transfers between devices  60.7 us (52%)
  starting transfers between devices  28.2 us (24%)
  Pallas kernels  26.5 us (23%)
    ppermute x9, waiting for transfers between devices, move(): return lax.ppermute(value, BOTH, pairs)  43.6 us
    pallas_call x13, Pallas kernels, call(): pl.pallas_call(kernel, out_shape=[jax.ShapeDtypeStruct(s, d) for s, d in...  26.5 us
    ppermute x25, waiting for transfers between devices, swap(): lax.ppermute(value, 'dp', [(source, source ^ bit) for source in range(DP)])  17.2 us
    ppermute x25, starting transfers between devices, swap(): lax.ppermute(value, 'dp', [(source, source ^ bit) for source in range(DP)])  16.9 us
    ppermute x9, starting transfers between devices, move(): return lax.ppermute(value, BOTH, pairs)  11.3 us
  transfers between devices with their start and end apart: 34, of which 13 were waited for; matrix products, arithmetic and copies ran while one was open for 0% of the time, Pallas kernels for 20%

profile of v2, /device:TPU:2, one launch (start us, length us, event | category | flops | bytes accessed | tf_op | source)
XLA Modules:
  0.0 116.5 jit_solution(9175044366667491690)
XLA Ops:
  0.7 1.7 %shard_map.101 = (bf16[384,384]{1,0:T(8,128)(2,1)S(1)}, bf16[384,384]{1,0:T(8,128)(2,1)S(1)}, bf16[768,384]{1,0:T(8,128)(2,1)S(1)}) custom-call(s32[1]{0:T(128)} %bitcast.3.place_ref, s32[1]{0:T(128)} %bitcast.place_1.place_ref, s32[1]{0:T(128)} %bitcast.1.place_2.place_ref, bf16[3072,128]{1,0:T(8,128)(2,1)} %rest_15_.2, bf16[3072,128]{1,0:T(8,128)(2,1)} %rest_16_.1, ...), custom_call_target="tpu_custom_call" | custom-call | flops 2000000000 | tf_op jit(solution)/shard_map/pallas_call | solution.py:95
  2.4 1.7 %collective-permute-start = (bf16[384,384]{1,0:T(8,128)(2,1)S(1)}, bf16[384,384]{1,0:T(8,128)(2,1)S(1)}, u32[]{:S(2)}, u32[]{:S(2)}) collective-permute-start(bf16[384,384]{1,0:T(8,128)(2,1)S(1)} %get-tuple-element.53), channel_id=1, source_target_pairs={{0,1},{1,2},{2,3},{3,4},{4,5},{5,6},{6,7},{7,8},{8,9},{9,10},{10,1... | collective-permute-start | bytes 884744 | tf_op jit(solution)/shard_map/ppermute | solution.py:38
  4.0 1.6 %collective-permute-start.1 = (bf16[384,384]{1,0:T(8,128)(2,1)S(1)}, bf16[384,384]{1,0:T(8,128)(2,1)S(1)}, u32[]{:S(2)}, u32[]{:S(2)}) collective-permute-start(bf16[384,384]{1,0:T(8,128)(2,1)S(1)} %get-tuple-element.54), channel_id=1, source_target_pairs={{0,1},{1,2},{2,3},{3,4},{4,5},{5,6},{6,7},{7,8},{8,9},{9,10},{10,1... | collective-permute-start | bytes 884744 | tf_op jit(solution)/shard_map/ppermute | solution.py:38
  5.6 3.0 %collective-permute-start.14 = (bf16[768,384]{1,0:T(8,128)(2,1)S(1)}, bf16[768,384]{1,0:T(8,128)(2,1)S(1)}, u32[]{:S(2)}, u32[]{:S(2)}) collective-permute-start(bf16[768,384]{1,0:T(8,128)(2,1)S(1)} %get-tuple-element.49.rest_0_), channel_id=1, source_target_pairs={{0,3},{1,0},{2,1},{3,2},{4,7},{5,4},{6,5},{7,6},{8,11},{9,8},{10,9... | collective-permute-start | bytes 1769480 | tf_op jit(solution)/shard_map/ppermute | solution.py:38
  8.6 5.0 %shard_map.102 = (bf16[256,3072]{1,0:T(8,128)(2,1)S(1)}, bf16[256,3072]{1,0:T(8,128)(2,1)S(1)}, f32[256,1]{1,0:T(8,128)S(1)}, bf16[256,128]{1,0:T(8,128)(2,1)S(1)}, bf16[256,256]{1,0:T(8,128)(2,1)S(1)}) custom-call(f32[1,3072]{1,0:T(1,128)S(1)} %bitcast.4, bf16[256,3072]{1,0:T(8,128)(2,1)} %rest_14_.3, bf16[256,3072]{1,0:T(8,128)(2,1)S(1)} %copy-done, ...), custom_call_target="tpu_custom_call" | custom-call | flops 4000000000 | tf_op jit(solution)/shard_map/pallas_call | solution.py:95
  13.6 5.9 %collective-permute-done.refs_0_ = bf16[384,384]{1,0:T(8,128)(2,1)S(1)} collective-permute-done((bf16[384,384]{1,0:T(8,128)(2,1)S(1)}, bf16[384,384]{1,0:T(8,128)(2,1)S(1)}, u32[]{:S(2)}, u32[]{:S(2)}) %collective-permute-start) | collective-permute-done | bytes 294944 | tf_op jit(solution)/shard_map/ppermute | solution.py:38
  19.5 1.9 %collective-permute-start.2 = (bf16[384,384]{1,0:T(8,128)(2,1)S(1)}, bf16[384,384]{1,0:T(8,128)(2,1)S(1)}, u32[]{:S(2)}, u32[]{:S(2)}) collective-permute-start(bf16[384,384]{1,0:T(8,128)(2,1)S(1)} %shard_map.103.rest_0_), channel_id=1, source_target_pairs={{0,128},{64,192},{128,0},{192,64},{1,129},{65,193},{129,1},{193,65... | collective-permute-start | bytes 884744 | tf_op jit(solution)/shard_map/ppermute | solution.py:42
  21.4 1.0 shard_map.104
  22.4 2.7 %collective-permute-done.1.refs_0_ = bf16[384,384]{1,0:T(8,128)(2,1)S(1)} collective-permute-done((bf16[384,384]{1,0:T(8,128)(2,1)S(1)}, bf16[384,384]{1,0:T(8,128)(2,1)S(1)}, u32[]{:S(2)}, u32[]{:S(2)}) %collective-permute-start.1) | collective-permute-done | bytes 294944 | tf_op jit(solution)/shard_map/ppermute | solution.py:38
  25.1 3.8 %collective-permute-done.2.refs_2_.rest_2_ = bf16[384,384]{1,0:T(8,128)(2,1)S(1)} collective-permute-done((bf16[384,384]{1,0:T(8,128)(2,1)S(1)}, bf16[384,384]{1,0:T(8,128)(2,1)S(1)}, u32[]{:S(2)}, u32[]{:S(2)}) %collective-permute-start.2) | collective-permute-done | bytes 294944 | tf_op jit(solution)/shard_map/ppermute | solution.py:42
  29.0 0.5 collective-permute-start.10
  29.5 1.8 %collective-permute-done.12.rest_5_.rest_0_.rest_8_ = bf16[384,384]{1,0:T(8,128)(2,1)S(1)} collective-permute-done((bf16[384,384]{1,0:T(8,128)(2,1)S(1)}, bf16[384,384]{1,0:T(8,128)(2,1)S(1)}, u32[]{:S(2)}, u32[]{:S(2)}) %collective-permute-start.12) | collective-permute-done | bytes 294944 | tf_op jit(solution)/shard_map/ppermute | solution.py:38
  31.3 2.8 %collective-permute-start.3 = (bf16[384,384]{1,0:T(8,128)(2,1)S(1)}, bf16[384,384]{1,0:T(8,128)(2,1)S(1)}, u32[]{:S(2)}, u32[]{:S(2)}) collective-permute-start(bf16[384,384]{1,0:T(8,128)(2,1)S(1)} %shard_map.105.rest_1_), channel_id=1, source_target_pairs={{0,128},{64,192},{128,0},{192,64},{1,129},{65,193},{129,1},{193,65... | collective-permute-start | bytes 884744 | tf_op jit(solution)/shard_map/ppermute | solution.py:42
  34.8 4.0 %collective-permute-done.3.rest_4_.rest_3_ = bf16[384,384]{1,0:T(8,128)(2,1)S(1)} collective-permute-done((bf16[384,384]{1,0:T(8,128)(2,1)S(1)}, bf16[384,384]{1,0:T(8,128)(2,1)S(1)}, u32[]{:S(2)}, u32[]{:S(2)}) %collective-permute-start.3) | collective-permute-done | bytes 294944 | tf_op jit(solution)/shard_map/ppermute | solution.py:42
  39.0 2.1 %collective-permute-start.23 = (bf16[384,768]{1,0:T(8,128)(2,1)S(1)}, bf16[384,768]{1,0:T(8,128)(2,1)S(1)}, u32[]{:S(2)}, u32[]{:S(2)}) collective-permute-start(bf16[384,768]{1,0:T(8,128)(2,1)S(1)} %get-tuple-element.61.rest_8_), channel_id=1, source_target_pairs={{0,128},{64,192},{128,0},{192,64},{1,129},{65,193},{129,1},{193,65... | collective-permute-start | bytes 1769480 | tf_op jit(solution)/shard_map/ppermute | solution.py:42
  41.1 6.7 %collective-permute-done.13.rest_9_.rest_1_ = bf16[384,384]{1,0:T(8,128)(2,1)S(1)} collective-permute-done((bf16[384,384]{1,0:T(8,128)(2,1)S(1)}, bf16[384,384]{1,0:T(8,128)(2,1)S(1)}, u32[]{:S(2)}, u32[]{:S(2)}) %collective-permute-start.13) | collective-permute-done | bytes 294944 | tf_op jit(solution)/shard_map/ppermute | solution.py:38
  47.9 2.5 %shard_map.107 = (bf16[256,128]{1,0:T(8,128)(2,1)S(1)}, bf16[256,256]{1,0:T(8,128)(2,1)S(1)}, bf16[384,384]{1,0:T(8,128)(2,1)S(1)}, bf16[384,384]{1,0:T(8,128)(2...) custom-call(s32[1]{0:T(128)} %bitcast.place_1.place_ref, ...), custom_call_target="tpu_custom_call" | custom-call | flops 4000000000 | tf_op jit(solution)/shard_map/pallas_call | solution.py:95
  50.9 6.7 %collective-permute-done.15.rest_2_.rest_10_ = bf16[768,384]{1,0:T(8,128)(2,1)S(1)} collective-permute-done((bf16[768,384]{1,0:T(8,128)(2,1)S(1)}, bf16[768,384]{1,0:T(8,128)(2,1)S(1)}, u32[]{:S(2)}, u32[]{:S(2)}) %collective-permute-start.15) | collective-permute-done | bytes 589856 | tf_op jit(solution)/shard_map/ppermute | solution.py:38
  58.7 1.3 %collective-permute-done.21.rest_2_ = bf16[384,384]{1,0:T(8,128)(2,1)S(1)} collective-permute-done((bf16[384,384]{1,0:T(8,128)(2,1)S(1)}, bf16[384,384]{1,0:T(8,128)(2,1)S(1)}, u32[]{:S(2)}, u32[]{:S(2)}) %collective-permute-start.21) | collective-permute-done | bytes 294944 | tf_op jit(solution)/shard_map/ppermute | solution.py:42
  60.6 3.3 %collective-permute-start.24 = (bf16[384,768]{1,0:T(8,128)(2,1)S(1)}, bf16[384,768]{1,0:T(8,128)(2,1)S(1)}, u32[]{:S(2)}, u32[]{:S(2)}) collective-permute-start(bf16[384,768]{1,0:T(8,128)(2,1)S(1)} %get-tuple-element.71), channel_id=1, source_target_pairs={{0,128},{64,192},{128,0},{192,64},{1,129},{65,193},{129,1},{193,65... | collective-permute-start | bytes 1769480 | tf_op jit(solution)/shard_map/ppermute | solution.py:42
  64.0 2.2 %shard_map.108 = (bf16[256,128]{1,0:T(8,128)(2,1)S(1)}, bf16[256,256]{1,0:T(8,128)(2,1)S(1)}, bf16[384,384]{1,0:T(8,128)(2,1)S(1)}, bf16[384,384]{1,0:T(8,128)(2...) custom-call(s32[1]{0:T(128)} %bitcast.1.place_2.place_ref, ...), custom_call_target="tpu_custom_call" | custom-call | flops 4000000000 | tf_op jit(solution)/shard_map/pallas_call | solution.py:95
  67.3 7.8 %shard_map.110 = (bf16[256,3072]{1,0:T(8,128)(2,1)}, f32[8,128]{1,0:T(8,128)S(1)}) custom-call(s32[1]{0:T(128)} %bitcast.place_1.place_ref, s32[1]{0:T(128)} %bitcast.1.place_2.place_ref, bf16[256,3072]{1,0:T(8,128)(2,1)S(1)} %get-tuple-element.52.cot, f32[1,3072]{1,0:T(1,128)S(1)} %bitcast.5, f32[256,1]{1,0:T(8,128)S(1)} %get-tuple-element.76.inverse_ref, ...), custom_call_target="tpu_custom_call" | custom-call | flops 5000000000 | tf_op jit(solution)/shard_map/pallas_call | solution.py:95
  75.2 2.4 %collective-permute-done.24.here_1 = bf16[384,768]{1,0:T(8,128)(2,1)S(1)} collective-permute-done((bf16[384,768]{1,0:T(8,128)(2,1)S(1)}, bf16[384,768]{1,0:T(8,128)(2,1)S(1)}, u32[]{:S(2)}, u32[]{:S(2)}) %collective-permute-start.24) | collective-permute-done | bytes 589856 | tf_op jit(solution)/shard_map/ppermute | solution.py:42
  77.9 1.8 %collective-permute-start.30 = (bf16[384,384]{1,0:T(8,128)(2,1)S(1)}, bf16[384,384]{1,0:T(8,128)(2,1)S(1)}, u32[]{:S(2)}, u32[]{:S(2)}) collective-permute-start(bf16[384,384]{1,0:T(8,128)(2,1)S(1)} %get-tuple-element.80.rest_16_), channel_id=1, source_target_pairs={{0,128},{64,192},{128,0},{192,64},{1,129},{65,193},{129,1},{193,65... | collective-permute-start | bytes 884744 | tf_op jit(solution)/shard_map/ppermute | solution.py:42
  79.7 3.3 %collective-permute-start.29 = (bf16[384,768]{1,0:T(8,128)(2,1)S(1)}, bf16[384,768]{1,0:T(8,128)(2,1)S(1)}, u32[]{:S(2)}, u32[]{:S(2)}) collective-permute-start(bf16[384,768]{1,0:T(8,128)(2,1)S(1)} %get-tuple-element.84), channel_id=1, source_target_pairs={{0,191},{1,0},{2,1},{3,2},{4,3},{5,4},{6,5},{7,6},{8,7},{9,8},{10,... | collective-permute-start | bytes 1769480 | tf_op jit(solution)/shard_map/ppermute | solution.py:38
  83.0 4.2 %shard_map.112 = (bf16[256,3072]{1,0:T(8,128)(2,1)}, f32[8,128]{1,0:T(8,128)S(1)}) custom-call(s32[1]{0:T(128)} %bitcast.place_1.place_ref, s32[1]{0:T(128)} %bitcast.1.place_2.place_ref, bf16[256,128]{1,0:T(8,128)(2,1)S(1)} %get-tuple-element.50.refs_1_.hidden.hidden_0, bf16[256,128]{1,0:T(8,128)(2,1)S(1)} %get-tuple-element.62.rest_6_.hidden_1, ...), custom_call_target="tpu_custom_call" | custom-call | flops 4000000000 | tf_op jit(solution)/shard_map/pallas_call | solution.py:95
  87.3 1.0 collective-permute-start.32
  88.3 1.7 %collective-permute-start.31 = (bf16[384,384]{1,0:T(8,128)(2,1)S(1)}, bf16[384,384]{1,0:T(8,128)(2,1)S(1)}, u32[]{:S(2)}, u32[]{:S(2)}) collective-permute-start(bf16[384,384]{1,0:T(8,128)(2,1)S(1)} %get-tuple-element.88), channel_id=1, source_target_pairs={{0,190},{1,191},{2,0},{3,1},{4,2},{5,3},{6,4},{7,5},{8,6},{9,7},{1... | collective-permute-start | bytes 884744 | tf_op jit(solution)/shard_map/ppermute | solution.py:38
  89.9 5.1 %collective-permute-done.32.arrived = bf16[384,384]{1,0:T(8,128)(2,1)S(1)} collective-permute-done((bf16[384,384]{1,0:T(8,128)(2,1)S(1)}, bf16[384,384]{1,0:T(8,128)(2,1)S(1)}, u32[]{:S(2)}, u32[]{:S(2)}) %collective-permute-start.32) | collective-permute-done | bytes 294944 | tf_op jit(solution)/shard_map/ppermute | solution.py:42
  95.0 11.6 %collective-permute-done.29.rest_0_.near = bf16[384,768]{1,0:T(8,128)(2,1)S(1)} collective-permute-done((bf16[384,768]{1,0:T(8,128)(2,1)S(1)}, bf16[384,768]{1,0:T(8,128)(2,1)S(1)}, u32[]{:S(2)}, u32[]{:S(2)}) %collective-permute-start.29) | collective-permute-done | bytes 589856 | tf_op jit(solution)/shard_map/ppermute | solution.py:38
  106.8 8.2 %collective-permute-done.33.high = bf16[384,384]{1,0:T(8,128)(2,1)S(1)} collective-permute-done((bf16[384,384]{1,0:T(8,128)(2,1)S(1)}, bf16[384,384]{1,0:T(8,128)(2,1)S(1)}, u32[]{:S(2)}, u32[]{:S(2)}) %collective-permute-start.33) | collective-permute-done | bytes 294944 | tf_op jit(solution)/shard_map/ppermute | solution.py:38
  115.0 1.3 %shard_map.115 = (f32[768,128]{1,0:T(8,128)}, f32[768,128]{1,0:T(8,128)}, f32[128,768]{1,0:T(8,128)}) custom-call(f32[384,768]{1,0:T(8,128)S(1)} %get-tuple-element.83.mine, bf16[384,768]{1,0:T(8,128)(2,1)S(1)} %collective-permute-done.23.rest_4_.here, bf16[384,768]{1,0:T(8,128)(2,1)S(1)} %collective-permute-done.29.rest_0_.near, ...), custom_call_target="tpu_custom_call" | custom-call | flops 2000000000 | tf_op jit(solution)/shard_map/pallas_call | solution.py:95
  (55 shorter events, 5.0 us)
Async XLA Ops:
  2.4 17.1 %collective-permute-start = (bf16[384,384]{1,0:T(8,128)(2,1)S(1)}, bf16[384,384]{1,0:T(8,128)(2,1)S(1)}, u32[]{:S(2)}, u32[]{:S(2)}) collective-permute-start(bf16[384,384]{1,0:T(8,128)(2,1)S(1)} %get-tuple-element.53), channel_id=1, source_target_pairs={{0,1},{1,2},{2,3},{3,4},{4,5},{5,6},{6,7},{7,8},{8,9},{9,10},{10,1... | collective-permute-start | bytes 884744 | tf_op jit(solution)/shard_map/ppermute | solution.py:38
  4.0 21.1 %collective-permute-start.1 = (bf16[384,384]{1,0:T(8,128)(2,1)S(1)}, bf16[384,384]{1,0:T(8,128)(2,1)S(1)}, u32[]{:S(2)}, u32[]{:S(2)}) collective-permute-start(bf16[384,384]{1,0:T(8,128)(2,1)S(1)} %get-tuple-element.54), channel_id=1, source_target_pairs={{0,1},{1,2},{2,3},{3,4},{4,5},{5,6},{6,7},{7,8},{8,9},{9,10},{10,1... | collective-permute-start | bytes 884744 | tf_op jit(solution)/shard_map/ppermute | solution.py:38
  5.6 23.4 %collective-permute-start.14 = (bf16[768,384]{1,0:T(8,128)(2,1)S(1)}, bf16[768,384]{1,0:T(8,128)(2,1)S(1)}, u32[]{:S(2)}, u32[]{:S(2)}) collective-permute-start(bf16[768,384]{1,0:T(8,128)(2,1)S(1)} %get-tuple-element.49.rest_0_), channel_id=1, source_target_pairs={{0,3},{1,0},{2,1},{3,2},{4,7},{5,4},{6,5},{7,6},{8,11},{9,8},{10,9... | collective-permute-start | bytes 1769480 | tf_op jit(solution)/shard_map/ppermute | solution.py:38
  19.5 11.8 %collective-permute-start.12 = (bf16[384,384]{1,0:T(8,128)(2,1)S(1)}, bf16[384,384]{1,0:T(8,128)(2,1)S(1)}, u32[]{:S(2)}, u32[]{:S(2)}) collective-permute-start(bf16[384,384]{1,0:T(8,128)(2,1)S(1)} %shard_map.103.rest_0_), channel_id=1, source_target_pairs={{0,1},{1,2},{2,3},{3,4},{4,5},{5,6},{6,7},{7,8},{8,9},{9,10},{10,1... | collective-permute-start | bytes 884744 | tf_op jit(solution)/shard_map/ppermute | solution.py:38
  19.5 14.6 %collective-permute-start.4 = (bf16[384,384]{1,0:T(8,128)(2,1)S(1)}, bf16[384,384]{1,0:T(8,128)(2,1)S(1)}, u32[]{:S(2)}, u32[]{:S(2)}) collective-permute-start(bf16[384,384]{1,0:T(8,128)(2,1)S(1)} %shard_map.103.rest_0_), channel_id=1, source_target_pairs={{0,64},{64,0},{128,192},{192,128},{1,65},{65,1},{129,193},{193,129... | collective-permute-start | bytes 884744 | tf_op jit(solution)/shard_map/ppermute | solution.py:42
  19.5 9.5 %collective-permute-start.2 = (bf16[384,384]{1,0:T(8,128)(2,1)S(1)}, bf16[384,384]{1,0:T(8,128)(2,1)S(1)}, u32[]{:S(2)}, u32[]{:S(2)}) collective-permute-start(bf16[384,384]{1,0:T(8,128)(2,1)S(1)} %shard_map.103.rest_0_), channel_id=1, source_target_pairs={{0,128},{64,192},{128,0},{192,64},{1,129},{65,193},{129,1},{193,65... | collective-permute-start | bytes 884744 | tf_op jit(solution)/shard_map/ppermute | solution.py:42
  25.1 9.0 %collective-permute-start.8 = (bf16[384,384]{1,0:T(8,128)(2,1)S(1)}, bf16[384,384]{1,0:T(8,128)(2,1)S(1)}, u32[]{:S(2)}, u32[]{:S(2)}) collective-permute-start(bf16[384,384]{1,0:T(8,128)(2,1)S(1)} %get-tuple-element.57), channel_id=1, source_target_pairs={{0,64},{64,0},{128,192},{192,128},{1,65},{65,1},{129,193},{193,129... | collective-permute-start | bytes 884744 | tf_op jit(solution)/shard_map/ppermute | solution.py:42
  29.0 5.6 %collective-permute-start.9 = (bf16[384,384]{1,0:T(8,128)(2,1)S(1)}, bf16[384,384]{1,0:T(8,128)(2,1)S(1)}, u32[]{:S(2)}, u32[]{:S(2)}) collective-permute-start(bf16[384,384]{1,0:T(8,128)(2,1)S(1)} %get-tuple-element.58), channel_id=1, source_target_pairs={{0,64},{64,0},{128,192},{192,128},{1,65},{65,1},{129,193},{193,129... | collective-permute-start | bytes 884744 | tf_op jit(solution)/shard_map/ppermute | solution.py:42
  29.0 5.6 %collective-permute-start.10 = (bf16[384,384]{1,0:T(8,128)(2,1)S(1)}, bf16[384,384]{1,0:T(8,128)(2,1)S(1)}, u32[]{:S(2)}, u32[]{:S(2)}) collective-permute-start(bf16[384,384]{1,0:T(8,128)(2,1)S(1)} %get-tuple-element.59), channel_id=1, source_target_pairs={{0,64},{64,0},{128,192},{192,128},{1,65},{65,1},{129,193},{193,129... | collective-permute-start | bytes 884744 | tf_op jit(solution)/shard_map/ppermute | solution.py:42
  31.3 7.5 %collective-permute-start.3 = (bf16[384,384]{1,0:T(8,128)(2,1)S(1)}, bf16[384,384]{1,0:T(8,128)(2,1)S(1)}, u32[]{:S(2)}, u32[]{:S(2)}) collective-permute-start(bf16[384,384]{1,0:T(8,128)(2,1)S(1)} %shard_map.105.rest_1_), channel_id=1, source_target_pairs={{0,128},{64,192},{128,0},{192,64},{1,129},{65,193},{129,1},{193,65... | collective-permute-start | bytes 884744 | tf_op jit(solution)/shard_map/ppermute | solution.py:42
  34.1 4.7 %collective-permute-start.11 = (bf16[384,384]{1,0:T(8,128)(2,1)S(1)}, bf16[384,384]{1,0:T(8,128)(2,1)S(1)}, u32[]{:S(2)}, u32[]{:S(2)}) collective-permute-start(bf16[384,384]{1,0:T(8,128)(2,1)S(1)} %get-tuple-element.60), channel_id=1, source_target_pairs={{0,64},{64,0},{128,192},{192,128},{1,65},{65,1},{129,193},{193,129... | collective-permute-start | bytes 884744 | tf_op jit(solution)/shard_map/ppermute | solution.py:42
  34.1 4.9 %collective-permute-start.6 = (bf16[384,384]{1,0:T(8,128)(2,1)S(1)}, bf16[384,384]{1,0:T(8,128)(2,1)S(1)}, u32[]{:S(2)}, u32[]{:S(2)}) collective-permute-start(bf16[384,384]{1,0:T(8,128)(2,1)S(1)} %collective-permute-done.2.refs_2_.rest_2_), channel_id=1, source_target_pairs={{0,64},{64,0},{128,192},{192,128},{1,65},{65,1},{129,193},{193,129... | collective-permute-start | bytes 884744 | tf_op jit(solution)/shard_map/ppermute | solution.py:42
  34.6 13.2 %collective-permute-start.13 = (bf16[384,384]{1,0:T(8,128)(2,1)S(1)}, bf16[384,384]{1,0:T(8,128)(2,1)S(1)}, u32[]{:S(2)}, u32[]{:S(2)}) collective-permute-start(bf16[384,384]{1,0:T(8,128)(2,1)S(1)} %shard_map.105.rest_1_), channel_id=1, source_target_pairs={{0,1},{1,2},{2,3},{3,4},{4,5},{5,6},{6,7},{7,8},{8,9},{9,10},{10,1... | collective-permute-start | bytes 884744 | tf_op jit(solution)/shard_map/ppermute | solution.py:38
  34.6 13.2 %collective-permute-start.5 = (bf16[384,384]{1,0:T(8,128)(2,1)S(1)}, bf16[384,384]{1,0:T(8,128)(2,1)S(1)}, u32[]{:S(2)}, u32[]{:S(2)}) collective-permute-start(bf16[384,384]{1,0:T(8,128)(2,1)S(1)} %shard_map.105.rest_1_), channel_id=1, source_target_pairs={{0,64},{64,0},{128,192},{192,128},{1,65},{65,1},{129,193},{193,129... | collective-permute-start | bytes 884744 | tf_op jit(solution)/shard_map/ppermute | solution.py:42
  38.8 9.0 %collective-permute-start.7 = (bf16[384,384]{1,0:T(8,128)(2,1)S(1)}, bf16[384,384]{1,0:T(8,128)(2,1)S(1)}, u32[]{:S(2)}, u32[]{:S(2)}) collective-permute-start(bf16[384,384]{1,0:T(8,128)(2,1)S(1)} %collective-permute-done.3.rest_4_.rest_3_), channel_id=1, source_target_pairs={{0,64},{64,0},{128,192},{192,128},{1,65},{65,1},{129,193},{193,129... | collective-permute-start | bytes 884744 | tf_op jit(solution)/shard_map/ppermute | solution.py:42
  38.8 18.7 %collective-permute-start.15 = (bf16[768,384]{1,0:T(8,128)(2,1)S(1)}, bf16[768,384]{1,0:T(8,128)(2,1)S(1)}, u32[]{:S(2)}, u32[]{:S(2)}) collective-permute-start(bf16[768,384]{1,0:T(8,128)(2,1)S(1)} %collective-permute-done.14), channel_id=1, source_target_pairs={{0,3},{1,4},{2,5},{3,2},{4,7},{5,8},{6,9},{7,6},{8,11},{9,12},{10,... | collective-permute-start | bytes 1769480 | tf_op jit(solution)/shard_map/ppermute | solution.py:38
  39.0 19.0 %collective-permute-start.23 = (bf16[384,768]{1,0:T(8,128)(2,1)S(1)}, bf16[384,768]{1,0:T(8,128)(2,1)S(1)}, u32[]{:S(2)}, u32[]{:S(2)}) collective-permute-start(bf16[384,768]{1,0:T(8,128)(2,1)S(1)} %get-tuple-element.61.rest_8_), channel_id=1, source_target_pairs={{0,128},{64,192},{128,0},{192,64},{1,129},{65,193},{129,1},{193,65... | collective-permute-start | bytes 1769480 | tf_op jit(solution)/shard_map/ppermute | solution.py:42
  50.3 7.8 %collective-permute-start.19 = (bf16[384,384]{1,0:T(8,128)(2,1)S(1)}, bf16[384,384]{1,0:T(8,128)(2,1)S(1)}, u32[]{:S(2)}, u32[]{:S(2)}) collective-permute-start(bf16[384,384]{1,0:T(8,128)(2,1)S(1)} %get-tuple-element.66), channel_id=1, source_target_pairs={{0,64},{64,0},{128,192},{192,128},{1,65},{65,1},{129,193},{193,129... | collective-permute-start | bytes 884744 | tf_op jit(solution)/shard_map/ppermute | solution.py:42
  50.4 8.2 %collective-permute-start.20 = (bf16[384,384]{1,0:T(8,128)(2,1)S(1)}, bf16[384,384]{1,0:T(8,128)(2,1)S(1)}, u32[]{:S(2)}, u32[]{:S(2)}) collective-permute-start(bf16[384,384]{1,0:T(8,128)(2,1)S(1)} %get-tuple-element.67), channel_id=1, source_target_pairs={{0,64},{64,0},{128,192},{192,128},{1,65},{65,1},{129,193},{193,129... | collective-permute-start | bytes 884744 | tf_op jit(solution)/shard_map/ppermute | solution.py:42
  57.6 6.4 %collective-permute-start.18 = (bf16[768,384]{1,0:T(8,128)(2,1)S(1)}, bf16[768,384]{1,0:T(8,128)(2,1)S(1)}, u32[]{:S(2)}, u32[]{:S(2)}) collective-permute-start(bf16[768,384]{1,0:T(8,128)(2,1)S(1)} %collective-permute-done.15.rest_2_.rest_10_), channel_id=1, source_target_pairs={{0,64},{64,0},{128,192},{192,128},{1,65},{65,1},{129,193},{193,129... | collective-permute-start | bytes 1769480 | tf_op jit(solution)/shard_map/ppermute | solution.py:42
  58.1 5.9 %collective-permute-start.16 = (bf16[384,384]{1,0:T(8,128)(2,1)S(1)}, bf16[384,384]{1,0:T(8,128)(2,1)S(1)}, u32[]{:S(2)}, u32[]{:S(2)}) collective-permute-start(bf16[384,384]{1,0:T(8,128)(2,1)S(1)} %collective-permute-done.12.rest_5_.rest_0_.rest_8_), channel_id=1, source_target_pairs={{0,64},{64,0},{128,192},{192,128},{1,65},{65,1},{129,193},{193,129... | collective-permute-start | bytes 884744 | tf_op jit(solution)/shard_map/ppermute | solution.py:42
  58.6 5.4 %collective-permute-start.17 = (bf16[384,384]{1,0:T(8,128)(2,1)S(1)}, bf16[384,384]{1,0:T(8,128)(2,1)S(1)}, u32[]{:S(2)}, u32[]{:S(2)}) collective-permute-start(bf16[384,384]{1,0:T(8,128)(2,1)S(1)} %collective-permute-done.13.rest_9_.rest_1_), channel_id=1, source_target_pairs={{0,64},{64,0},{128,192},{192,128},{1,65},{65,1},{129,193},{193,129... | collective-permute-start | bytes 884744 | tf_op jit(solution)/shard_map/ppermute | solution.py:42
  60.6 16.9 %collective-permute-start.24 = (bf16[384,768]{1,0:T(8,128)(2,1)S(1)}, bf16[384,768]{1,0:T(8,128)(2,1)S(1)}, u32[]{:S(2)}, u32[]{:S(2)}) collective-permute-start(bf16[384,768]{1,0:T(8,128)(2,1)S(1)} %get-tuple-element.71), channel_id=1, source_target_pairs={{0,128},{64,192},{128,0},{192,64},{1,129},{65,193},{129,1},{193,65... | collective-permute-start | bytes 1769480 | tf_op jit(solution)/shard_map/ppermute | solution.py:42
  66.2 8.9 %collective-permute-start.25 = (bf16[384,384]{1,0:T(8,128)(2,1)S(1)}, bf16[384,384]{1,0:T(8,128)(2,1)S(1)}, u32[]{:S(2)}, u32[]{:S(2)}) collective-permute-start(bf16[384,384]{1,0:T(8,128)(2,1)S(1)} %get-tuple-element.72), channel_id=1, source_target_pairs={{0,64},{64,0},{128,192},{192,128},{1,65},{65,1},{129,193},{193,129... | collective-permute-start | bytes 884744 | tf_op jit(solution)/shard_map/ppermute | solution.py:42
  66.3 8.8 %collective-permute-start.26 = (bf16[384,384]{1,0:T(8,128)(2,1)S(1)}, bf16[384,384]{1,0:T(8,128)(2,1)S(1)}, u32[]{:S(2)}, u32[]{:S(2)}) collective-permute-start(bf16[384,384]{1,0:T(8,128)(2,1)S(1)} %get-tuple-element.73), channel_id=1, source_target_pairs={{0,64},{64,0},{128,192},{192,128},{1,65},{65,1},{129,193},{193,129... | collective-permute-start | bytes 884744 | tf_op jit(solution)/shard_map/ppermute | solution.py:42
  66.8 8.3 %collective-permute-start.27 = (bf16[384,384]{1,0:T(8,128)(2,1)S(1)}, bf16[384,384]{1,0:T(8,128)(2,1)S(1)}, u32[]{:S(2)}, u32[]{:S(2)}) collective-permute-start(bf16[384,384]{1,0:T(8,128)(2,1)S(1)} %get-tuple-element.74), channel_id=1, source_target_pairs={{0,64},{64,0},{128,192},{192,128},{1,65},{65,1},{129,193},{193,129... | collective-permute-start | bytes 884744 | tf_op jit(solution)/shard_map/ppermute | solution.py:42
  66.9 8.2 %collective-permute-start.28 = (bf16[384,384]{1,0:T(8,128)(2,1)S(1)}, bf16[384,384]{1,0:T(8,128)(2,1)S(1)}, u32[]{:S(2)}, u32[]{:S(2)}) collective-permute-start(bf16[384,384]{1,0:T(8,128)(2,1)S(1)} %get-tuple-element.75), channel_id=1, source_target_pairs={{0,64},{64,0},{128,192},{192,128},{1,65},{65,1},{129,193},{193,129... | collective-permute-start | bytes 884744 | tf_op jit(solution)/shard_map/ppermute | solution.py:42
  77.9 9.3 %collective-permute-start.30 = (bf16[384,384]{1,0:T(8,128)(2,1)S(1)}, bf16[384,384]{1,0:T(8,128)(2,1)S(1)}, u32[]{:S(2)}, u32[]{:S(2)}) collective-permute-start(bf16[384,384]{1,0:T(8,128)(2,1)S(1)} %get-tuple-element.80.rest_16_), channel_id=1, source_target_pairs={{0,128},{64,192},{128,0},{192,64},{1,129},{65,193},{129,1},{193,65... | collective-permute-start | bytes 884744 | tf_op jit(solution)/shard_map/ppermute | solution.py:42
  79.7 26.9 %collective-permute-start.29 = (bf16[384,768]{1,0:T(8,128)(2,1)S(1)}, bf16[384,768]{1,0:T(8,128)(2,1)S(1)}, u32[]{:S(2)}, u32[]{:S(2)}) collective-permute-start(bf16[384,768]{1,0:T(8,128)(2,1)S(1)} %get-tuple-element.84), channel_id=1, source_target_pairs={{0,191},{1,0},{2,1},{3,2},{4,3},{5,4},{6,5},{7,6},{8,7},{9,8},{10,... | collective-permute-start | bytes 1769480 | tf_op jit(solution)/shard_map/ppermute | solution.py:38
  87.3 7.8 %collective-permute-start.32 = (bf16[384,384]{1,0:T(8,128)(2,1)S(1)}, bf16[384,384]{1,0:T(8,128)(2,1)S(1)}, u32[]{:S(2)}, u32[]{:S(2)}) collective-permute-start(bf16[384,384]{1,0:T(8,128)(2,1)S(1)} %get-tuple-element.89), channel_id=1, source_target_pairs={{0,128},{64,192},{128,0},{192,64},{1,129},{65,193},{129,1},{193,65... | collective-permute-start | bytes 884744 | tf_op jit(solution)/shard_map/ppermute | solution.py:42
  88.3 18.5 %collective-permute-start.31 = (bf16[384,384]{1,0:T(8,128)(2,1)S(1)}, bf16[384,384]{1,0:T(8,128)(2,1)S(1)}, u32[]{:S(2)}, u32[]{:S(2)}) collective-permute-start(bf16[384,384]{1,0:T(8,128)(2,1)S(1)} %get-tuple-element.88), channel_id=1, source_target_pairs={{0,190},{1,191},{2,0},{3,1},{4,2},{5,3},{6,4},{7,5},{8,6},{9,7},{1... | collective-permute-start | bytes 884744 | tf_op jit(solution)/shard_map/ppermute | solution.py:38
  106.7 8.3 %collective-permute-start.33 = (bf16[384,384]{1,0:T(8,128)(2,1)S(1)}, bf16[384,384]{1,0:T(8,128)(2,1)S(1)}, u32[]{:S(2)}, u32[]{:S(2)}) collective-permute-start(bf16[384,384]{1,0:T(8,128)(2,1)S(1)} %shard_map.114), channel_id=1, source_target_pairs={{0,190},{1,191},{2,0},{3,1},{4,2},{5,3},{6,4},{7,5},{8,6},{9,7},{1... | collective-permute-start | bytes 884744 | tf_op jit(solution)/shard_map/ppermute | solution.py:38
  (4 other events, 20.6 us)

commit v3 on v2

--- a/solution.py
+++ b/solution.py
@@ -8,6 +8,7 @@
 from jax.sharding import PartitionSpec as P
 
 DP = 4
+PIECES = 3
 RING = 4
 TIE_LIMIT = 1024 * 1024
 VMEM_LIMIT = 12 * 1024 * 1024
@@ -105,7 +106,7 @@
     )(*[v[None] for v in scalars], *operands, *far, *tokens)
 
 
-def after(value, *tokens):
+def after(value, *tokens, micros=0):
     anywhere = pl.BlockSpec(memory_space=pl.ANY)
     return pl.pallas_call(
         lambda *refs: None,
@@ -114,7 +115,9 @@
         out_specs=anywhere,
         input_output_aliases={0: 0},
         compiler_params=pltpu.CompilerParams(vmem_limit_bytes=TIE_LIMIT),
-        cost_estimate=pl.CostEstimate(flops=0, bytes_accessed=0, transcendentals=0),
+        cost_estimate=pl.CostEstimate(
+            flops=int(micros * 10**9), bytes_accessed=0, transcendentals=0
+        ),
     )(value, *tokens)
 
 
@@ -144,40 +147,35 @@
 
 
 def write_terms(place, part, units, hidden, delta, normed, cot, send, keep):
-    half = part // 2
+    size = part // PIECES
     for k in (1, 3, 0, 2):
-        for side in range(2):
-            at = columns(place, part, k, side * half, half)
+        for side in range(PIECES):
+            at = columns(place, part, k, side * size, size)
+            start = k // 2 * part + side * size
+            out = keep
             if k % 2:
-                out = send[k // 2 * 2 + side]
-                into = slice(0, half)
-            else:
-                out = keep
-                into = slice(k // 2 * part + side * half, k // 2 * part + (side + 1) * half)
+                out = send[start // (2 * size)]
+                start = start % (2 * size)
+            into = slice(start, start + size)
             out[:2 * units, into] = mul(delta, normed[:, at], TN).astype(out.dtype)
             out[2 * units:, into] = mul(hidden, cot[:, at], TN).astype(out.dtype)
 
 
-def pack_kernel(part, units, place_ref, place_1, place_2, gate, up, down, low, high, other, gates, ups, downs, sems):
+def pack_kernel(part, units, place_ref, place_1, place_2, gate, up, down, *rest):
+    outs, (gates, ups, downs, sems) = rest[:2], rest[2:]
     place = place_ref[0]
-    half = part // 2
     sources, targets = [], []
     for i, k in enumerate((0, 2)):
         at = columns(place, part, k, 0, part)
         sources += [gate.at[at, :], up.at[at, :], down.at[:, at]]
         targets += [gates.at[i], ups.at[i], downs.at[i]]
     copies = fetch(sources, targets, sems)
-    for copy in copies[:3]:
-        copy.wait()
-    for out, start in ((low, 0), (high, half)):
-        out[:, :units] = gates[0, start:start + half, :]
-        out[:, units:2 * units] = ups[0, start:start + half, :]
-        out[:, 2 * units:] = jnp.transpose(downs[0, :, start:start + half])
-    for copy in copies[3:]:
-        copy.wait()
-    other[:, :units] = gates[1]
-    other[:, units:2 * units] = ups[1]
-    other[:, 2 * units:] = jnp.transpose(downs[1])
+    for i, out in enumerate(outs):
+        for copy in copies[3 * i:3 * i + 3]:
+            copy.wait()
+        out[:, :units] = gates[i]
+        out[:, units:2 * units] = ups[i]
+        out[:, 2 * units:] = jnp.transpose(downs[i])
 
 
 def own_kernel(gain, tokens_far, cot_far, gate_far, up_far, down_far, *rest):
@@ -207,14 +205,14 @@
 
 def terms_kernel(part, units, place_ref, normed, cot, hidden, delta, *rest):
     write_terms(
-        place_ref[0], part, units, hidden[...], delta[...], normed, cot, rest[-5:-1], rest[-1]
+        place_ref[0], part, units, hidden[...], delta[...], normed, cot, rest[-PIECES - 1:-1], rest[-1]
     )
 
 
 def shard_kernel(part, units, layout, place_ref, normed, cot, *rest):
     pieces = rest[:len(layout)]
-    hidden_ref, delta_ref = rest[-7:-5]
-    send, keep = rest[-5:-1], rest[-1]
+    hidden_ref, delta_ref = rest[-PIECES - 3:-PIECES - 1]
+    send, keep = rest[-PIECES - 1:-1], rest[-1]
     place = place_ref[0]
     pre = None
     grad = None
@@ -231,28 +229,28 @@
 
 
 def summed(part, keep, arrived):
-    half = part // 2
-    return [keep[:, i * half:(i + 1) * half] + arrived[i][...].astype(jnp.float32) for i in range(DP)]
+    size = 2 * part // PIECES
+    total = [
+        keep[:, i * size:(i + 1) * size] + arrived[i][...].astype(jnp.float32)
+        for i in range(PIECES)
+    ]
+    return jnp.concatenate(total, axis=1)
 
 
 def add_kernel(part, keep, *rest):
-    half = part // 2
-    total = summed(part, keep, rest[:DP])
+    total = summed(part, keep, rest[:PIECES])
     out, mine = rest[-2:]
-    mine[:, :half] = total[0]
-    mine[:, half:] = total[1]
-    out[:, :half] = total[2].astype(jnp.bfloat16)
-    out[:, half:] = total[3].astype(jnp.bfloat16)
+    mine[...] = total[:, :part]
+    out[...] = total[:, part:].astype(jnp.bfloat16)
 
 
 def last_add_kernel(part, keep, mine_1, here_1, *rest):
     half = part // 2
-    total = summed(part, keep, rest[:DP])
+    total = summed(part, keep, rest[:PIECES])
     low, high, mine, near = rest[-4:]
-    mine[:, :half] = total[0]
-    mine[:, half:] = total[1]
-    low[...] = total[2].astype(jnp.bfloat16)
-    high[...] = total[3].astype(jnp.bfloat16)
+    mine[...] = total[:, :part]
+    low[...] = total[:, part:part + half].astype(jnp.bfloat16)
+    high[...] = total[:, part + half:].astype(jnp.bfloat16)
     near[...] = (mine_1[...] + here_1[...].astype(jnp.float32)).astype(jnp.bfloat16)
 
 
@@ -375,67 +373,57 @@
     gain = norm_gain[None, :]
     dma = pltpu.SemaphoreType.DMA
 
-    low, high, other = call(
-        functools.partial(pack_kernel, part, units), [],
-        [((half, width), bf16)] * 2 + [((part, width), bf16)], 2, far=weights,
-        scalars=(place, place_1, place_2),
+    piece, other = call(
+        functools.partial(pack_kernel, part, units), [], [((part, width), bf16)] * 2, 2,
+        far=weights, scalars=(place, place_1, place_2),
         scratch=[pltpu.VMEM((2, part, units), bf16)] * 2
         + [pltpu.VMEM((2, units, part), bf16), dma((6,))],
     )
-    one_a = forward(low)
-    one_b = forward(high)
+    one = forward(piece)
     two_z = around_first(other)
 
     acts = [((rows, units), bf16), ((rows, 2 * units), bf16)]
-    terms = [((width, half), bf16)] * 4 + [((width, 2 * part), f32)]
+    terms = [((width, 2 * part // PIECES), bf16)] * PIECES + [((width, 2 * part), f32)]
 
     cot, normed, inverse, hidden_0, delta_0 = call(
-        own_kernel, [gain], [((rows, model), bf16)] * 2 + [((rows, 1), f32)] + acts, 4,
+        own_kernel, [gain], [((rows, model), bf16)] * 2 + [((rows, 1), f32)] + acts, 5,
         far=[tokens, cotangent] + weights, tokens=(other,),
         scratch=[pltpu.VMEM((rows, model), bf16)] + [pltpu.VMEM((model, units), bf16)] * 2
         + [pltpu.VMEM((units, model), bf16), dma((5,))],
     )
 
-    one_a = after(one_a, hidden_0)
     *send, keep = call(
-        functools.partial(terms_kernel, part, units), [normed, cot, hidden_0, delta_0], terms, 3,
-        scalars=(place,), tokens=(one_a,),
-    )
-    one_xa = swap(one_a, 2)
-    two_a = forward(one_a)
-    one_b = after(one_b, keep, one_xa)
-    one_xb = swap(one_b, 2)
-    two_b = forward(one_b)
-    two_z = around_second(two_z)
-    ones = [one_a, one_b, one_xa, one_xb]
-    ones = ones + [swap(v, 1) for v in ones]
-    layout_1 = [(k, start, half) for k in (0, 2, 1, 3) for start in (0, half)]
-    twos = [two_a, two_b, two_z]
-    twos = twos + [swap(v, 1) for v in twos]
-    layout_2 = [(0, 0, half), (0, half, half), (2, 0, part), (1, 0, half), (1, half, half), (3, 0, part)]
-
+        functools.partial(terms_kernel, part, units), [normed, cot, hidden_0, delta_0], terms, 5,
+        scalars=(place,),
+    )
     def add(keep, send, tokens=()):
         return call(
             functools.partial(add_kernel, part), [keep] + [swap(v, 1) for v in send],
             [((width, part), bf16), ((width, part), f32)], 1, tokens=tokens,
         )
 
-    out_0, mine_0 = add(keep, send, (one_xb, two_a))
+    out_0, mine_0 = add(keep, send)
     here_0 = swap(out_0, 2)
+    one = after(one, out_0, two_z)
+    one_x = swap(one, 2)
+    two = forward(one)
+    two_z = around_second(two_z)
+    ones = [one, one_x, swap(one, 1), swap(one_x, 1)]
+    twos = [two, two_z, swap(two, 1), swap(two_z, 1)]
+    layout = [(k, 0, part) for k in (0, 2, 1, 3)]
 
     hidden_1, delta_1, *send, keep = call(
-        functools.partial(shard_kernel, part, units, layout_1), [normed, cot] + ones,
-        acts + terms, 4, scalars=(place_1,), tokens=(out_0, two_b),
-    )
-    out_1, mine_1 = add(keep, send, (here_0,))
-    here_1 = swap(out_1, 2)
+        functools.partial(shard_kernel, part, units, layout), [normed, cot] + ones,
+        acts + terms, 4, scalars=(place_1,), tokens=(out_0, two, two_z),
+    )
+    keep_1, send_1 = keep, send
 
     hidden_2, delta_2, *send, keep = call(
-        functools.partial(shard_kernel, part, units, layout_2), [normed, cot] + twos,
+        functools.partial(shard_kernel, part, units, layout), [normed, cot] + twos,
         acts + terms, 4, scalars=(place_2,), tokens=(hidden_1,),
     )
     input_grad, flag_backward = call(
-        functools.partial(backward_out_kernel, part, units, (layout_1, layout_2)),
+        functools.partial(backward_out_kernel, part, units, (layout, layout)),
         [cot, gain, inverse, delta_0, delta_1, delta_2] + ones + twos,
         [((rows, model), bf16)], 5,
         far=[tokens, gate_weight, up_weight], scalars=(place_1, place_2), direct=True, flag=True,
@@ -446,16 +434,19 @@
         ],
     )
 
+    here_0 = after(here_0, hidden_1, micros=14)
+    out_1, mine_1 = add(keep_1, send_1, (here_0,))
+    here_1 = swap(out_1, 2)
     low_2, high_2, mine_2, near = call(
         functools.partial(last_add_kernel, part),
         [keep, mine_1, here_1] + [swap(v, 1) for v in send],
         [((width, half), bf16)] * 2 + [((width, part), f32), ((width, part), bf16)], 1,
         tokens=(flag_backward,),
     )
-    near = backward(near)
+    near = after(backward(near), micros=8)
 
     block_out, flag_forward = call(
-        functools.partial(forward_out_kernel, part, units, (layout_1, layout_2)),
+        functools.partial(forward_out_kernel, part, units, (layout, layout)),
         [hidden_0, hidden_1, hidden_2] + ones + twos, [((rows, model), bf16)], 4,
         far=[tokens, down_weight], tokens=(low_2,), scalars=(place_1, place_2), direct=True, flag=True,
         scratch=[
@@ -470,7 +461,7 @@
     sum_low = back_two(sum_low)
     sum_high, = call(
         functools.partial(hop_kernel, half), [mine_2, swap(high_2, 2)],
-        [((width, half), bf16)], 0.5, tokens=(near,),
+        [((width, half), bf16)], 0.5,
     )
     sum_high = back_two(sum_high)
 

time: 117 us -> 106 us (0.906)
  starting transfers between devices: 28.2 us -> 21.9 us
  waiting for transfers between devices: 60.7 us -> 57.7 us
  Pallas kernels: 26.5 us -> 25 us
    ppermute x9 -> x7, waiting for transfers between devices: 43.6 us -> 25.8 us  [move(): return lax.ppermute(value, BOTH, pairs)]
    ppermute x25 -> x18, waiting for transfers between devices: 17.2 us -> 31.9 us  [swap(): lax.ppermute(value, 'dp', [(source, source ^ bit) for source in range(DP)])]
    ppermute x25 -> x18, starting transfers between devices: 16.9 us -> 11.1 us  [swap(): lax.ppermute(value, 'dp', [(source, source ^ bit) for source in range(DP)])]
    pallas_call x13, Pallas kernels: 26.5 us -> 25 us  [call(): pl.pallas_call(kernel, out_shape=[jax.ShapeDtypeStruct(s, d) for s, d in...]
    ppermute x9 -> x7, starting transfers between devices: 11.3 us -> 10.8 us  [move(): return lax.ppermute(value, BOTH, pairs)]
  transfers between devices with their start and end apart: 34 -> 25, of which waited for: 13 -> 14; matrix products, arithmetic and copies ran while one was open for 0% -> 0% of each run, Pallas kernels for 20% -> 21%
where the time goes in v3:
time: 106 us
  waiting for transfers between devices  57.7 us (54%)
  Pallas kernels  25 us (24%)
  starting transfers between devices  21.9 us (21%)
    ppermute x18, waiting for transfers between devices, swap(): lax.ppermute(value, 'dp', [(source, source ^ bit) for source in range(DP)])  31.9 us
    ppermute x7, waiting for transfers between devices, move(): return lax.ppermute(value, BOTH, pairs)  25.8 us
    pallas_call x13, Pallas kernels, call(): pl.pallas_call(kernel, out_shape=[jax.ShapeDtypeStruct(s, d) for s, d in...  25 us
    ppermute x18, starting transfers between devices, swap(): lax.ppermute(value, 'dp', [(source, source ^ bit) for source in range(DP)])  11.1 us
    ppermute x7, starting transfers between devices, move(): return lax.ppermute(value, BOTH, pairs)  10.8 us
  transfers between devices with their start and end apart: 25, of which 14 were waited for; matrix products, arithmetic and copies ran while one was open for 0% of the time, Pallas kernels for 21%

profile of v3, /device:TPU:2, one launch (start us, length us, event | category | flops | bytes accessed | tf_op | source)
XLA Modules:
  0.0 105.5 jit_solution(17681786034483782800)
XLA Ops:
  0.7 1.7 %shard_map.101 = (bf16[768,384]{1,0:T(8,128)(2,1)S(1)}, bf16[768,384]{1,0:T(8,128)(2,1)S(1)}) custom-call(s32[1]{0:T(128)} %bitcast.3.place_ref, s32[1]{0:T(128)} %bitcast.place_1.place_ref, s32[1]{0:T(128)} %bitcast.1.place_2.place_ref, bf16[3072,128]{1,0:T(8,128)(2,1)} %rest_9_.2, bf16[3072,128]{1,0:T(8,128)(2,1)} %rest_10_.1, bf16[128,3072]{1,0:T(8,128)(2,1)} %rest_9_.3), custom_call_target="tpu_custom_call" | custom-call | flops 2000000000 | tf_op jit(solution)/shard_map/pallas_call | solution.py:96
  2.4 1.7 %collective-permute-start = (bf16[768,384]{1,0:T(8,128)(2,1)S(1)}, bf16[768,384]{1,0:T(8,128)(2,1)S(1)}, u32[]{:S(2)}, u32[]{:S(2)}) collective-permute-start(bf16[768,384]{1,0:T(8,128)(2,1)S(1)} %get-tuple-element.49), channel_id=1, source_target_pairs={{0,1},{1,2},{2,3},{3,4},{4,5},{5,6},{6,7},{7,8},{8,9},{9,10},{10,1... | collective-permute-start | bytes 1769480 | tf_op jit(solution)/shard_map/ppermute | solution.py:39
  4.0 3.0 %collective-permute-start.4 = (bf16[768,384]{1,0:T(8,128)(2,1)S(1)}, bf16[768,384]{1,0:T(8,128)(2,1)S(1)}, u32[]{:S(2)}, u32[]{:S(2)}) collective-permute-start(bf16[768,384]{1,0:T(8,128)(2,1)S(1)} %get-tuple-element.45.rest_0_), channel_id=1, source_target_pairs={{0,3},{1,0},{2,1},{3,2},{4,7},{5,4},{6,5},{7,6},{8,11},{9,8},{10,9... | collective-permute-start | bytes 1769480 | tf_op jit(solution)/shard_map/ppermute | solution.py:39
  7.0 5.0 %shard_map.102 = (bf16[256,3072]{1,0:T(8,128)(2,1)S(1)}, bf16[256,3072]{1,0:T(8,128)(2,1)S(1)}, f32[256,1]{1,0:T(8,128)S(1)}, bf16[256,128]{1,0:T(8,128)(2,1)S(1)}, bf16[256,256]{1,0:T(8,128)(2,1)S(1)}) custom-call(f32[1,3072]{1,0:T(1,128)S(1)} %bitcast.4, bf16[256,3072]{1,0:T(8,128)(2,1)} %rest_8_.3, bf16[256,3072]{1,0:T(8,128)(2,1)S(1)} %copy-done, ...), custom_call_target="tpu_custom_call" | custom-call | flops 5000000000 | tf_op jit(solution)/shard_map/pallas_call | solution.py:96
  12.0 0.8 shard_map.103
  13.5 1.1 %collective-permute-done.1.rest_0_ = bf16[384,512]{1,0:T(8,128)(2,1)S(1)} collective-permute-done((bf16[384,512]{1,0:T(8,128)(2,1)S(1)}, bf16[384,512]{1,0:T(8,128)(2,1)S(1)}, u32[]{:S(2)}, u32[]{:S(2)}) %collective-permute-start.1) | collective-permute-done | bytes 393248 | tf_op jit(solution)/shard_map/ppermute | solution.py:43
  14.6 0.6 collective-permute-done.2.rest_1_
  15.2 0.6 collective-permute-done.3.rest_2_
  16.0 9.0 %collective-permute-done.refs_0_ = bf16[768,384]{1,0:T(8,128)(2,1)S(1)} collective-permute-done((bf16[768,384]{1,0:T(8,128)(2,1)S(1)}, bf16[768,384]{1,0:T(8,128)(2,1)S(1)}, u32[]{:S(2)}, u32[]{:S(2)}) %collective-permute-start) | collective-permute-done | bytes 589856 | tf_op jit(solution)/shard_map/ppermute | solution.py:39
  25.0 1.8 %collective-permute-start.5 = (bf16[768,384]{1,0:T(8,128)(2,1)S(1)}, bf16[768,384]{1,0:T(8,128)(2,1)S(1)}, u32[]{:S(2)}, u32[]{:S(2)}) collective-permute-start(bf16[768,384]{1,0:T(8,128)(2,1)S(1)} %shard_map.105.rest_0_), channel_id=1, source_target_pairs={{0,128},{64,192},{128,0},{192,64},{1,129},{65,193},{129,1},{193,65... | collective-permute-start | bytes 1769480 | tf_op jit(solution)/shard_map/ppermute | solution.py:43
  26.8 12.8 %collective-permute-done.5.rest_1_ = bf16[768,384]{1,0:T(8,128)(2,1)S(1)} collective-permute-done((bf16[768,384]{1,0:T(8,128)(2,1)S(1)}, bf16[768,384]{1,0:T(8,128)(2,1)S(1)}, u32[]{:S(2)}, u32[]{:S(2)}) %collective-permute-start.5) | collective-permute-done | bytes 589856 | tf_op jit(solution)/shard_map/ppermute | solution.py:43
  39.6 1.7 %collective-permute-start.15 = (bf16[384,768]{1,0:T(8,128)(2,1)S(1)}, bf16[384,768]{1,0:T(8,128)(2,1)S(1)}, u32[]{:S(2)}, u32[]{:S(2)}) collective-permute-start(bf16[384,768]{1,0:T(8,128)(2,1)S(1)} %get-tuple-element.55.refs_1_.rest_4_), channel_id=1, source_target_pairs={{0,128},{64,192},{128,0},{192,64},{1,129},{65,193},{129,1},{193,65... | collective-permute-start | bytes 1769480 | tf_op jit(solution)/shard_map/ppermute | solution.py:43
  41.3 2.7 %collective-permute-done.9.rest_6_.rest_1_.rest_5_ = bf16[768,384]{1,0:T(8,128)(2,1)S(1)} collective-permute-done((bf16[768,384]{1,0:T(8,128)(2,1)S(1)}, bf16[768,384]{1,0:T(8,128)(2,1)S(1)}, u32[]{:S(2)}, u32[]{:S(2)}) %collective-permute-start.9) | collective-permute-done | bytes 589856 | tf_op jit(solution)/shard_map/ppermute | solution.py:39
  44.0 1.2 %collective-permute-done.8.rest_5_.rest_0_.rest_4_ = bf16[768,384]{1,0:T(8,128)(2,1)S(1)} collective-permute-done((bf16[768,384]{1,0:T(8,128)(2,1)S(1)}, bf16[768,384]{1,0:T(8,128)(2,1)S(1)}, u32[]{:S(2)}, u32[]{:S(2)}) %collective-permute-start.8) | collective-permute-done | bytes 589856 | tf_op jit(solution)/shard_map/ppermute | solution.py:39
  45.3 1.8 %shard_map.106 = (bf16[256,128]{1,0:T(8,128)(2,1)S(1)}, bf16[256,256]{1,0:T(8,128)(2,1)S(1)}, bf16[384,512]{1,0:T(8,128)(2,1)S(1)}, bf16[384,512]{1,0:T(8,128)(2...) custom-call(s32[1]{0:T(128)} %bitcast.place_1.place_ref, bf16[256,3072]{1,0:T(8,128)(2,1)S(1)} %get-tuple-element.47.normed, ...), custom_call_target="tpu_custom_call" | custom-call | flops 4000000000 | tf_op jit(solution)/shard_map/pallas_call | solution.py:96
  47.1 0.6 collective-permute-start.12
  47.8 7.5 %collective-permute-done.15.refs_0_ = bf16[384,768]{1,0:T(8,128)(2,1)S(1)} collective-permute-done((bf16[384,768]{1,0:T(8,128)(2,1)S(1)}, bf16[384,768]{1,0:T(8,128)(2,1)S(1)}, u32[]{:S(2)}, u32[]{:S(2)}) %collective-permute-start.15) | collective-permute-done | bytes 589856 | tf_op jit(solution)/shard_map/ppermute | solution.py:43
  55.3 1.7 %collective-permute-done.14.rest_2_ = bf16[384,512]{1,0:T(8,128)(2,1)S(1)} collective-permute-done((bf16[384,512]{1,0:T(8,128)(2,1)S(1)}, bf16[384,512]{1,0:T(8,128)(2,1)S(1)}, u32[]{:S(2)}, u32[]{:S(2)}) %collective-permute-start.14) | collective-permute-done | bytes 393248 | tf_op jit(solution)/shard_map/ppermute | solution.py:43
  57.3 1.8 %collective-permute-start.16 = (bf16[384,768]{1,0:T(8,128)(2,1)S(1)}, bf16[384,768]{1,0:T(8,128)(2,1)S(1)}, u32[]{:S(2)}, u32[]{:S(2)}) collective-permute-start(bf16[384,768]{1,0:T(8,128)(2,1)S(1)} %get-tuple-element.64), channel_id=1, source_target_pairs={{0,128},{64,192},{128,0},{192,64},{1,129},{65,193},{129,1},{193,65... | collective-permute-start | bytes 1769480 | tf_op jit(solution)/shard_map/ppermute | solution.py:43
  59.1 1.8 %shard_map.107 = (bf16[256,128]{1,0:T(8,128)(2,1)S(1)}, bf16[256,256]{1,0:T(8,128)(2,1)S(1)}, bf16[384,512]{1,0:T(8,128)(2,1)S(1)}, bf16[384,512]{1,0:T(8,128)(2...) custom-call(s32[1]{0:T(128)} %bitcast.1.place_2.place_ref, ...), custom_call_target="tpu_custom_call" | custom-call | flops 4000000000 | tf_op jit(solution)/shard_map/pallas_call | solution.py:96
  61.7 7.7 %shard_map.110 = (bf16[256,3072]{1,0:T(8,128)(2,1)}, f32[8,128]{1,0:T(8,128)S(1)}) custom-call(s32[1]{0:T(128)} %bitcast.place_1.place_ref, s32[1]{0:T(128)} %bitcast.1.place_2.place_ref, bf16[256,3072]{1,0:T(8,128)(2,1)S(1)} %get-tuple-element.48.cot, f32[1,3072]{1,0:T(1,128)S(1)} %bitcast.5, f32[256,1]{1,0:T(8,128)S(1)} %get-tuple-element.68.inverse_ref, ...), custom_call_target="tpu_custom_call" | custom-call | flops 5000000000 | tf_op jit(solution)/shard_map/pallas_call | solution.py:96
  69.4 3.3 %collective-permute-done.16.here_1 = bf16[384,768]{1,0:T(8,128)(2,1)S(1)} collective-permute-done((bf16[384,768]{1,0:T(8,128)(2,1)S(1)}, bf16[384,768]{1,0:T(8,128)(2,1)S(1)}, u32[]{:S(2)}, u32[]{:S(2)}) %collective-permute-start.16) | collective-permute-done | bytes 589856 | tf_op jit(solution)/shard_map/ppermute | solution.py:43
  73.0 1.8 %collective-permute-start.21 = (bf16[384,384]{1,0:T(8,128)(2,1)S(1)}, bf16[384,384]{1,0:T(8,128)(2,1)S(1)}, u32[]{:S(2)}, u32[]{:S(2)}) collective-permute-start(bf16[384,384]{1,0:T(8,128)(2,1)S(1)} %get-tuple-element.72.rest_10_), channel_id=1, source_target_pairs={{0,128},{64,192},{128,0},{192,64},{1,129},{65,193},{129,1},{193,65... | collective-permute-start | bytes 884744 | tf_op jit(solution)/shard_map/ppermute | solution.py:43
  74.9 2.1 %collective-permute-start.20 = (bf16[384,768]{1,0:T(8,128)(2,1)S(1)}, bf16[384,768]{1,0:T(8,128)(2,1)S(1)}, u32[]{:S(2)}, u32[]{:S(2)}) collective-permute-start(bf16[384,768]{1,0:T(8,128)(2,1)S(1)} %get-tuple-element.76), channel_id=1, source_target_pairs={{0,191},{1,0},{2,1},{3,2},{4,3},{5,4},{6,5},{7,6},{8,7},{9,8},{10,... | collective-permute-start | bytes 1769480 | tf_op jit(solution)/shard_map/ppermute | solution.py:39
  77.0 3.9 %shard_map.112 = (bf16[256,3072]{1,0:T(8,128)(2,1)}, f32[8,128]{1,0:T(8,128)S(1)}) custom-call(s32[1]{0:T(128)} %bitcast.place_1.place_ref, s32[1]{0:T(128)} %bitcast.1.place_2.place_ref, bf16[256,128]{1,0:T(8,128)(2,1)S(1)} %get-tuple-element.46.hidden.hidden_0, bf16[256,128]{1,0:T(8,128)(2,1)S(1)} %get-tuple-element.56.rest_4_.refs_1_.hidden_1, ...), custom_call_target="tpu_custom_call" | custom-call | flops 4000000000 | tf_op jit(solution)/shard_map/pallas_call | solution.py:96
  81.5 1.8 %collective-permute-start.23 = (bf16[384,384]{1,0:T(8,128)(2,1)S(1)}, bf16[384,384]{1,0:T(8,128)(2,1)S(1)}, u32[]{:S(2)}, u32[]{:S(2)}) collective-permute-start(bf16[384,384]{1,0:T(8,128)(2,1)S(1)} %get-tuple-element.81), channel_id=1, source_target_pairs={{0,128},{64,192},{128,0},{192,64},{1,129},{65,193},{129,1},{193,65... | collective-permute-start | bytes 884744 | tf_op jit(solution)/shard_map/ppermute | solution.py:43
  83.3 1.7 %collective-permute-start.22 = (bf16[384,384]{1,0:T(8,128)(2,1)S(1)}, bf16[384,384]{1,0:T(8,128)(2,1)S(1)}, u32[]{:S(2)}, u32[]{:S(2)}) collective-permute-start(bf16[384,384]{1,0:T(8,128)(2,1)S(1)} %get-tuple-element.80), channel_id=1, source_target_pairs={{0,190},{1,191},{2,0},{3,1},{4,2},{5,3},{6,4},{7,5},{8,6},{9,7},{1... | collective-permute-start | bytes 884744 | tf_op jit(solution)/shard_map/ppermute | solution.py:39
  85.0 3.9 %collective-permute-done.23.arrived = bf16[384,384]{1,0:T(8,128)(2,1)S(1)} collective-permute-done((bf16[384,384]{1,0:T(8,128)(2,1)S(1)}, bf16[384,384]{1,0:T(8,128)(2,1)S(1)}, u32[]{:S(2)}, u32[]{:S(2)}) %collective-permute-start.23) | collective-permute-done | bytes 294944 | tf_op jit(solution)/shard_map/ppermute | solution.py:43
  88.9 2.3 %collective-permute-start.24 = (bf16[384,384]{1,0:T(8,128)(2,1)S(1)}, bf16[384,384]{1,0:T(8,128)(2,1)S(1)}, u32[]{:S(2)}, u32[]{:S(2)}) collective-permute-start(bf16[384,384]{1,0:T(8,128)(2,1)S(1)} %shard_map.115), channel_id=1, source_target_pairs={{0,190},{1,191},{2,0},{3,1},{4,2},{5,3},{6,4},{7,5},{8,6},{9,7},{1... | collective-permute-start | bytes 884744 | tf_op jit(solution)/shard_map/ppermute | solution.py:39
  91.2 10.6 %collective-permute-done.20.refs_0_ = bf16[384,768]{1,0:T(8,128)(2,1)S(1)} collective-permute-done((bf16[384,768]{1,0:T(8,128)(2,1)S(1)}, bf16[384,768]{1,0:T(8,128)(2,1)S(1)}, u32[]{:S(2)}, u32[]{:S(2)}) %collective-permute-start.20) | collective-permute-done | bytes 589856 | tf_op jit(solution)/shard_map/ppermute | solution.py:39
  101.8 2.3 %collective-permute-done.24.high = bf16[384,384]{1,0:T(8,128)(2,1)S(1)} collective-permute-done((bf16[384,384]{1,0:T(8,128)(2,1)S(1)}, bf16[384,384]{1,0:T(8,128)(2,1)S(1)}, u32[]{:S(2)}, u32[]{:S(2)}) %collective-permute-start.24) | collective-permute-done | bytes 294944 | tf_op jit(solution)/shard_map/ppermute | solution.py:39
  104.1 1.3 %shard_map.116 = (f32[768,128]{1,0:T(8,128)}, f32[768,128]{1,0:T(8,128)}, f32[128,768]{1,0:T(8,128)}) custom-call(f32[384,768]{1,0:T(8,128)S(1)} %get-tuple-element.75.mine, bf16[384,768]{1,0:T(8,128)(2,1)S(1)} %shard_map.108.rest_3_.here, bf16[384,768]{1,0:T(8,128)(2,1)S(1)} %shard_map.113.near, bf16[384,384]{1,0:T(8,128)(2,1)S(1)} %collective-permute-done.22.low, ...), custom_call_target="tpu_custom_call" | custom-call | flops 2000000000 | tf_op jit(solution)/shard_map/pallas_call | solution.py:96
  (38 shorter events, 2.9 us)
Async XLA Ops:
  0.7 6.4 %copy-start = (bf16[256,3072]{1,0:T(8,128)(2,1)S(1)}, bf16[256,3072]{1,0:T(8,128)(2,1)}, u32[]{:S(2)}) copy-start(bf16[256,3072]{1,0:T(8,128)(2,1)} %cot_far.1) | copy-start | bytes 4718596
  0.7 6.4 %copy-start.1 = (f32[3072]{0:T(1024)S(1)}, f32[3072]{0:T(1024)}, u32[]{:S(2)}) copy-start(f32[3072]{0:T(1024)} %param.8) | copy-start | bytes 36868
  2.4 22.6 %collective-permute-start = (bf16[768,384]{1,0:T(8,128)(2,1)S(1)}, bf16[768,384]{1,0:T(8,128)(2,1)S(1)}, u32[]{:S(2)}, u32[]{:S(2)}) collective-permute-start(bf16[768,384]{1,0:T(8,128)(2,1)S(1)} %get-tuple-element.49), channel_id=1, source_target_pairs={{0,1},{1,2},{2,3},{3,4},{4,5},{5,6},{6,7},{7,8},{8,9},{9,10},{10,1... | collective-permute-start | bytes 1769480 | tf_op jit(solution)/shard_map/ppermute | solution.py:39
  4.0 21.0 %collective-permute-start.4 = (bf16[768,384]{1,0:T(8,128)(2,1)S(1)}, bf16[768,384]{1,0:T(8,128)(2,1)S(1)}, u32[]{:S(2)}, u32[]{:S(2)}) collective-permute-start(bf16[768,384]{1,0:T(8,128)(2,1)S(1)} %get-tuple-element.45.rest_0_), channel_id=1, source_target_pairs={{0,3},{1,0},{2,1},{3,2},{4,7},{5,4},{6,5},{7,6},{8,11},{9,8},{10,9... | collective-permute-start | bytes 1769480 | tf_op jit(solution)/shard_map/ppermute | solution.py:39
  12.8 1.8 %collective-permute-start.1 = (bf16[384,512]{1,0:T(8,128)(2,1)S(1)}, bf16[384,512]{1,0:T(8,128)(2,1)S(1)}, u32[]{:S(2)}, u32[]{:S(2)}) collective-permute-start(bf16[384,512]{1,0:T(8,128)(2,1)S(1)} %get-tuple-element.52), channel_id=1, source_target_pairs={{0,64},{64,0},{128,192},{192,128},{1,65},{65,1},{129,193},{193,129... | collective-permute-start | bytes 1179656 | tf_op jit(solution)/shard_map/ppermute | solution.py:43
  12.9 2.3 %collective-permute-start.2 = (bf16[384,512]{1,0:T(8,128)(2,1)S(1)}, bf16[384,512]{1,0:T(8,128)(2,1)S(1)}, u32[]{:S(2)}, u32[]{:S(2)}) collective-permute-start(bf16[384,512]{1,0:T(8,128)(2,1)S(1)} %get-tuple-element.53), channel_id=1, source_target_pairs={{0,64},{64,0},{128,192},{192,128},{1,65},{65,1},{129,193},{193,129... | collective-permute-start | bytes 1179656 | tf_op jit(solution)/shard_map/ppermute | solution.py:43
  13.4 2.3 %collective-permute-start.3 = (bf16[384,512]{1,0:T(8,128)(2,1)S(1)}, bf16[384,512]{1,0:T(8,128)(2,1)S(1)}, u32[]{:S(2)}, u32[]{:S(2)}) collective-permute-start(bf16[384,512]{1,0:T(8,128)(2,1)S(1)} %get-tuple-element.54), channel_id=1, source_target_pairs={{0,64},{64,0},{128,192},{192,128},{1,65},{65,1},{129,193},{193,129... | collective-permute-start | bytes 1179656 | tf_op jit(solution)/shard_map/ppermute | solution.py:43
  25.0 14.6 %collective-permute-start.5 = (bf16[768,384]{1,0:T(8,128)(2,1)S(1)}, bf16[768,384]{1,0:T(8,128)(2,1)S(1)}, u32[]{:S(2)}, u32[]{:S(2)}) collective-permute-start(bf16[768,384]{1,0:T(8,128)(2,1)S(1)} %shard_map.105.rest_0_), channel_id=1, source_target_pairs={{0,128},{64,192},{128,0},{192,64},{1,129},{65,193},{129,1},{193,65... | collective-permute-start | bytes 1769480 | tf_op jit(solution)/shard_map/ppermute | solution.py:43
  26.8 17.2 %collective-permute-start.9 = (bf16[768,384]{1,0:T(8,128)(2,1)S(1)}, bf16[768,384]{1,0:T(8,128)(2,1)S(1)}, u32[]{:S(2)}, u32[]{:S(2)}) collective-permute-start(bf16[768,384]{1,0:T(8,128)(2,1)S(1)} %collective-permute-done.4.refs_2_), channel_id=1, source_target_pairs={{0,3},{1,4},{2,5},{3,2},{4,7},{5,8},{6,9},{7,6},{8,11},{9,12},{10,... | collective-permute-start | bytes 1769480 | tf_op jit(solution)/shard_map/ppermute | solution.py:39
  26.8 18.5 %collective-permute-start.8 = (bf16[768,384]{1,0:T(8,128)(2,1)S(1)}, bf16[768,384]{1,0:T(8,128)(2,1)S(1)}, u32[]{:S(2)}, u32[]{:S(2)}) collective-permute-start(bf16[768,384]{1,0:T(8,128)(2,1)S(1)} %shard_map.105.rest_0_), channel_id=1, source_target_pairs={{0,1},{1,2},{2,3},{3,4},{4,5},{5,6},{6,7},{7,8},{8,9},{9,10},{10,1... | collective-permute-start | bytes 1769480 | tf_op jit(solution)/shard_map/ppermute | solution.py:39
  26.8 18.5 %collective-permute-start.6 = (bf16[768,384]{1,0:T(8,128)(2,1)S(1)}, bf16[768,384]{1,0:T(8,128)(2,1)S(1)}, u32[]{:S(2)}, u32[]{:S(2)}) collective-permute-start(bf16[768,384]{1,0:T(8,128)(2,1)S(1)} %shard_map.105.rest_0_), channel_id=1, source_target_pairs={{0,64},{64,0},{128,192},{192,128},{1,65},{65,1},{129,193},{193,129... | collective-permute-start | bytes 1769480 | tf_op jit(solution)/shard_map/ppermute | solution.py:43
  39.6 5.7 %collective-permute-start.7 = (bf16[768,384]{1,0:T(8,128)(2,1)S(1)}, bf16[768,384]{1,0:T(8,128)(2,1)S(1)}, u32[]{:S(2)}, u32[]{:S(2)}) collective-permute-start(bf16[768,384]{1,0:T(8,128)(2,1)S(1)} %collective-permute-done.5.rest_1_), channel_id=1, source_target_pairs={{0,64},{64,0},{128,192},{192,128},{1,65},{65,1},{129,193},{193,129... | collective-permute-start | bytes 1769480 | tf_op jit(solution)/shard_map/ppermute | solution.py:43
  39.6 15.7 %collective-permute-start.15 = (bf16[384,768]{1,0:T(8,128)(2,1)S(1)}, bf16[384,768]{1,0:T(8,128)(2,1)S(1)}, u32[]{:S(2)}, u32[]{:S(2)}) collective-permute-start(bf16[384,768]{1,0:T(8,128)(2,1)S(1)} %get-tuple-element.55.refs_1_.rest_4_), channel_id=1, source_target_pairs={{0,128},{64,192},{128,0},{192,64},{1,129},{65,193},{129,1},{193,65... | collective-permute-start | bytes 1769480 | tf_op jit(solution)/shard_map/ppermute | solution.py:43
  44.0 15.1 %collective-permute-start.11 = (bf16[768,384]{1,0:T(8,128)(2,1)S(1)}, bf16[768,384]{1,0:T(8,128)(2,1)S(1)}, u32[]{:S(2)}, u32[]{:S(2)}) collective-permute-start(bf16[768,384]{1,0:T(8,128)(2,1)S(1)} %collective-permute-done.9.rest_6_.rest_1_.rest_5_), channel_id=1, source_target_pairs={{0,64},{64,0},{128,192},{192,128},{1,65},{65,1},{129,193},{193,129... | collective-permute-start | bytes 1769480 | tf_op jit(solution)/shard_map/ppermute | solution.py:43
  45.3 13.9 %collective-permute-start.10 = (bf16[768,384]{1,0:T(8,128)(2,1)S(1)}, bf16[768,384]{1,0:T(8,128)(2,1)S(1)}, u32[]{:S(2)}, u32[]{:S(2)}) collective-permute-start(bf16[768,384]{1,0:T(8,128)(2,1)S(1)} %collective-permute-done.8.rest_5_.rest_0_.rest_4_), channel_id=1, source_target_pairs={{0,64},{64,0},{128,192},{192,128},{1,65},{65,1},{129,193},{193,129... | collective-permute-start | bytes 1769480 | tf_op jit(solution)/shard_map/ppermute | solution.py:43
  47.1 8.2 %collective-permute-start.12 = (bf16[384,512]{1,0:T(8,128)(2,1)S(1)}, bf16[384,512]{1,0:T(8,128)(2,1)S(1)}, u32[]{:S(2)}, u32[]{:S(2)}) collective-permute-start(bf16[384,512]{1,0:T(8,128)(2,1)S(1)} %get-tuple-element.60), channel_id=1, source_target_pairs={{0,64},{64,0},{128,192},{192,128},{1,65},{65,1},{129,193},{193,129... | collective-permute-start | bytes 1179656 | tf_op jit(solution)/shard_map/ppermute | solution.py:43
  47.7 7.6 %collective-permute-start.13 = (bf16[384,512]{1,0:T(8,128)(2,1)S(1)}, bf16[384,512]{1,0:T(8,128)(2,1)S(1)}, u32[]{:S(2)}, u32[]{:S(2)}) collective-permute-start(bf16[384,512]{1,0:T(8,128)(2,1)S(1)} %get-tuple-element.61), channel_id=1, source_target_pairs={{0,64},{64,0},{128,192},{192,128},{1,65},{65,1},{129,193},{193,129... | collective-permute-start | bytes 1179656 | tf_op jit(solution)/shard_map/ppermute | solution.py:43
  55.3 1.7 %collective-permute-start.14 = (bf16[384,512]{1,0:T(8,128)(2,1)S(1)}, bf16[384,512]{1,0:T(8,128)(2,1)S(1)}, u32[]{:S(2)}, u32[]{:S(2)}) collective-permute-start(bf16[384,512]{1,0:T(8,128)(2,1)S(1)} %get-tuple-element.62), channel_id=1, source_target_pairs={{0,64},{64,0},{128,192},{192,128},{1,65},{65,1},{129,193},{193,129... | collective-permute-start | bytes 1179656 | tf_op jit(solution)/shard_map/ppermute | solution.py:43
  57.3 15.5 %collective-permute-start.16 = (bf16[384,768]{1,0:T(8,128)(2,1)S(1)}, bf16[384,768]{1,0:T(8,128)(2,1)S(1)}, u32[]{:S(2)}, u32[]{:S(2)}) collective-permute-start(bf16[384,768]{1,0:T(8,128)(2,1)S(1)} %get-tuple-element.64), channel_id=1, source_target_pairs={{0,128},{64,192},{128,0},{192,64},{1,129},{65,193},{129,1},{193,65... | collective-permute-start | bytes 1769480 | tf_op jit(solution)/shard_map/ppermute | solution.py:43
  61.0 8.4 %collective-permute-start.17 = (bf16[384,512]{1,0:T(8,128)(2,1)S(1)}, bf16[384,512]{1,0:T(8,128)(2,1)S(1)}, u32[]{:S(2)}, u32[]{:S(2)}) collective-permute-start(bf16[384,512]{1,0:T(8,128)(2,1)S(1)} %get-tuple-element.65), channel_id=1, source_target_pairs={{0,64},{64,0},{128,192},{192,128},{1,65},{65,1},{129,193},{193,129... | collective-permute-start | bytes 1179656 | tf_op jit(solution)/shard_map/ppermute | solution.py:43
  61.1 8.3 %collective-permute-start.18 = (bf16[384,512]{1,0:T(8,128)(2,1)S(1)}, bf16[384,512]{1,0:T(8,128)(2,1)S(1)}, u32[]{:S(2)}, u32[]{:S(2)}) collective-permute-start(bf16[384,512]{1,0:T(8,128)(2,1)S(1)} %get-tuple-element.66), channel_id=1, source_target_pairs={{0,64},{64,0},{128,192},{192,128},{1,65},{65,1},{129,193},{193,129... | collective-permute-start | bytes 1179656 | tf_op jit(solution)/shard_map/ppermute | solution.py:43
  61.6 7.8 %collective-permute-start.19 = (bf16[384,512]{1,0:T(8,128)(2,1)S(1)}, bf16[384,512]{1,0:T(8,128)(2,1)S(1)}, u32[]{:S(2)}, u32[]{:S(2)}) collective-permute-start(bf16[384,512]{1,0:T(8,128)(2,1)S(1)} %get-tuple-element.67), channel_id=1, source_target_pairs={{0,64},{64,0},{128,192},{192,128},{1,65},{65,1},{129,193},{193,129... | collective-permute-start | bytes 1179656 | tf_op jit(solution)/shard_map/ppermute | solution.py:43
  73.0 8.3 %collective-permute-start.21 = (bf16[384,384]{1,0:T(8,128)(2,1)S(1)}, bf16[384,384]{1,0:T(8,128)(2,1)S(1)}, u32[]{:S(2)}, u32[]{:S(2)}) collective-permute-start(bf16[384,384]{1,0:T(8,128)(2,1)S(1)} %get-tuple-element.72.rest_10_), channel_id=1, source_target_pairs={{0,128},{64,192},{128,0},{192,64},{1,129},{65,193},{129,1},{193,65... | collective-permute-start | bytes 884744 | tf_op jit(solution)/shard_map/ppermute | solution.py:43
  74.9 26.9 %collective-permute-start.20 = (bf16[384,768]{1,0:T(8,128)(2,1)S(1)}, bf16[384,768]{1,0:T(8,128)(2,1)S(1)}, u32[]{:S(2)}, u32[]{:S(2)}) collective-permute-start(bf16[384,768]{1,0:T(8,128)(2,1)S(1)} %get-tuple-element.76), channel_id=1, source_target_pairs={{0,191},{1,0},{2,1},{3,2},{4,3},{5,4},{6,5},{7,6},{8,7},{9,8},{10,... | collective-permute-start | bytes 1769480 | tf_op jit(solution)/shard_map/ppermute | solution.py:39
  81.5 7.4 %collective-permute-start.23 = (bf16[384,384]{1,0:T(8,128)(2,1)S(1)}, bf16[384,384]{1,0:T(8,128)(2,1)S(1)}, u32[]{:S(2)}, u32[]{:S(2)}) collective-permute-start(bf16[384,384]{1,0:T(8,128)(2,1)S(1)} %get-tuple-element.81), channel_id=1, source_target_pairs={{0,128},{64,192},{128,0},{192,64},{1,129},{65,193},{129,1},{193,65... | collective-permute-start | bytes 884744 | tf_op jit(solution)/shard_map/ppermute | solution.py:43
  83.3 18.5 %collective-permute-start.22 = (bf16[384,384]{1,0:T(8,128)(2,1)S(1)}, bf16[384,384]{1,0:T(8,128)(2,1)S(1)}, u32[]{:S(2)}, u32[]{:S(2)}) collective-permute-start(bf16[384,384]{1,0:T(8,128)(2,1)S(1)} %get-tuple-element.80), channel_id=1, source_target_pairs={{0,190},{1,191},{2,0},{3,1},{4,2},{5,3},{6,4},{7,5},{8,6},{9,7},{1... | collective-permute-start | bytes 884744 | tf_op jit(solution)/shard_map/ppermute | solution.py:39
  88.9 15.1 %collective-permute-start.24 = (bf16[384,384]{1,0:T(8,128)(2,1)S(1)}, bf16[384,384]{1,0:T(8,128)(2,1)S(1)}, u32[]{:S(2)}, u32[]{:S(2)}) collective-permute-start(bf16[384,384]{1,0:T(8,128)(2,1)S(1)} %shard_map.115), channel_id=1, source_target_pairs={{0,190},{1,191},{2,0},{3,1},{4,2},{5,3},{6,4},{7,5},{8,6},{9,7},{1... | collective-permute-start | bytes 884744 | tf_op jit(solution)/shard_map/ppermute | solution.py:39

commit v4 on v3

--- a/solution.py
+++ b/solution.py
@@ -244,6 +244,15 @@
     out[...] = total[:, part:].astype(jnp.bfloat16)
 
 
+def split_add_kernel(part, keep, *rest):
+    half = part // 2
+    total = summed(part, keep, rest[:PIECES])
+    low, high, mine = rest[-3:]
+    mine[...] = total[:, :part]
+    low[...] = total[:, part:part + half].astype(jnp.bfloat16)
+    high[...] = total[:, part + half:].astype(jnp.bfloat16)
+
+
 def last_add_kernel(part, keep, mine_1, here_1, *rest):
     half = part // 2
     total = summed(part, keep, rest[:PIECES])
@@ -265,11 +274,11 @@
     out[...] = total.astype(jnp.bfloat16)
 
 
-def final_kernel(units, mine, here, near, low, high, gate, up, down, keep_g, keep_u, keep_d, sems):
+def final_kernel(units, mine, here_low, here_high, near, low, high, gate, up, down, keep_g, keep_u, keep_d, sems):
     half = low.shape[1]
-    for start, last in ((0, low), (half, high)):
+    for start, here, last in ((0, here_low, low), (half, here_high, high)):
         at = slice(start, start + half)
-        total = mine[:, at] + here[:, at].astype(jnp.float32) + near[:, at].astype(jnp.float32)
+        total = mine[:, at] + here[...].astype(jnp.float32) + near[:, at].astype(jnp.float32)
         total = (total + last[...].astype(jnp.float32)) * grad_scale
         keep_g[at, :] = jnp.transpose(total[:units])
         keep_u[at, :] = jnp.transpose(total[units:2 * units])
@@ -402,9 +411,12 @@
             [((width, part), bf16), ((width, part), f32)], 1, tokens=tokens,
         )
 
-    out_0, mine_0 = add(keep, send)
-    here_0 = swap(out_0, 2)
-    one = after(one, out_0, two_z)
+    low_0, high_0, mine_0 = call(
+        functools.partial(split_add_kernel, part), [keep] + [swap(v, 1) for v in send],
+        [((width, half), bf16)] * 2 + [((width, part), f32)], 1,
+    )
+    here_low = swap(low_0, 2)
+    one = after(one, low_0, two_z)
     one_x = swap(one, 2)
     two = forward(one)
     two_z = around_second(two_z)
@@ -414,7 +426,7 @@
 
     hidden_1, delta_1, *send, keep = call(
         functools.partial(shard_kernel, part, units, layout), [normed, cot] + ones,
-        acts + terms, 4, scalars=(place_1,), tokens=(out_0, two, two_z),
+        acts + terms, 4, scalars=(place_1,), tokens=(low_0, two, two_z),
     )
     keep_1, send_1 = keep, send
 
@@ -434,8 +446,8 @@
         ],
     )
 
-    here_0 = after(here_0, hidden_1, micros=14)
-    out_1, mine_1 = add(keep_1, send_1, (here_0,))
+    here_low = after(here_low, hidden_1, micros=14)
+    out_1, mine_1 = add(keep_1, send_1, (here_low,))
     here_1 = swap(out_1, 2)
     low_2, high_2, mine_2, near = call(
         functools.partial(last_add_kernel, part),
@@ -463,10 +475,11 @@
         functools.partial(hop_kernel, half), [mine_2, swap(high_2, 2)],
         [((width, half), bf16)], 0.5,
     )
+    here_high = swap(after(high_0, sum_high), 2)
     sum_high = back_two(sum_high)
 
     gate_grad, up_grad, down_grad = call(
-        functools.partial(final_kernel, units), [mine_0, here_0, near, sum_low, sum_high],
+        functools.partial(final_kernel, units), [mine_0, here_low, here_high, near, sum_low, sum_high],
         [((part, units), f32)] * 2 + [((units, part), f32)], 2, direct=True,
         scratch=[pltpu.VMEM((part, units), f32)] * 2 + [pltpu.VMEM((units, part), f32), dma((3,))],
     )

time: 106 us -> 99.4 us (0.938)
  waiting for transfers between devices: 57.7 us -> 49.6 us
  starting transfers between devices: 21.9 us -> 23.7 us
    ppermute x18 -> x19, waiting for transfers between devices: 31.9 us -> 25.6 us  [swap(): lax.ppermute(value, 'dp', [(source, source ^ bit) for source in range(DP)])]
    ppermute x18 -> x19, starting transfers between devices: 11.1 us -> 12.9 us  [swap(): lax.ppermute(value, 'dp', [(source, source ^ bit) for source in range(DP)])]
    ppermute x7, waiting for transfers between devices: 25.8 us -> 24 us  [move(): return lax.ppermute(value, BOTH, pairs)]
  transfers between devices with their start and end apart: 25 -> 26, of which waited for: 14 -> 16; matrix products, arithmetic and copies ran while one was open for 0% -> 0% of each run, Pallas kernels for 21% -> 22%
where the time goes in v4:
time: 99.4 us; the launch traced here: 99.2 us
  waiting for transfers between devices  49.6 us (50%)
  Pallas kernels  24.9 us (25%)
  starting transfers between devices  23.7 us (24%)
  between operations  1 us (1%)
    ppermute x19, waiting for transfers between devices, swap(): lax.ppermute(value, 'dp', [(source, source ^ bit) for source in range(DP)])  25.6 us
    pallas_call x13, Pallas kernels, call(): pl.pallas_call(kernel, out_shape=[jax.ShapeDtypeStruct(s, d) for s, d in...  24.9 us
    ppermute x7, waiting for transfers between devices, move(): return lax.ppermute(value, BOTH, pairs)  24 us
    ppermute x19, starting transfers between devices, swap(): lax.ppermute(value, 'dp', [(source, source ^ bit) for source in range(DP)])  12.9 us
    ppermute x7, starting transfers between devices, move(): return lax.ppermute(value, BOTH, pairs)  10.8 us
  transfers between devices with their start and end apart: 26, of which 16 were waited for; matrix products, arithmetic and copies ran while one was open for 0% of the time, Pallas kernels for 22%

profile of v4, /device:TPU:2, one launch (start us, length us, event | category | flops | bytes accessed | tf_op | source)
XLA Modules:
  0.0 99.2 jit_solution(8995039920212007413)
XLA Ops:
  0.7 1.7 %shard_map.101 = (bf16[768,384]{1,0:T(8,128)(2,1)S(1)}, bf16[768,384]{1,0:T(8,128)(2,1)S(1)}) custom-call(s32[1]{0:T(128)} %bitcast.3.place_ref, s32[1]{0:T(128)} %bitcast.place_1.place_ref, s32[1]{0:T(128)} %bitcast.1.place_2.place_ref, bf16[3072,128]{1,0:T(8,128)(2,1)} %rest_9_.2, bf16[3072,128]{1,0:T(8,128)(2,1)} %rest_10_.1, bf16[128,3072]{1,0:T(8,128)(2,1)} %rest_9_.3), custom_call_target="tpu_custom_call" | custom-call | flops 2000000000 | tf_op jit(solution)/shard_map/pallas_call | solution.py:96
  2.4 1.7 %collective-permute-start = (bf16[768,384]{1,0:T(8,128)(2,1)S(1)}, bf16[768,384]{1,0:T(8,128)(2,1)S(1)}, u32[]{:S(2)}, u32[]{:S(2)}) collective-permute-start(bf16[768,384]{1,0:T(8,128)(2,1)S(1)} %get-tuple-element.50), channel_id=1, source_target_pairs={{0,1},{1,2},{2,3},{3,4},{4,5},{5,6},{6,7},{7,8},{8,9},{9,10},{10,1... | collective-permute-start | bytes 1769480 | tf_op jit(solution)/shard_map/ppermute | solution.py:39
  4.0 3.0 %collective-permute-start.4 = (bf16[768,384]{1,0:T(8,128)(2,1)S(1)}, bf16[768,384]{1,0:T(8,128)(2,1)S(1)}, u32[]{:S(2)}, u32[]{:S(2)}) collective-permute-start(bf16[768,384]{1,0:T(8,128)(2,1)S(1)} %get-tuple-element.46.rest_0_), channel_id=1, source_target_pairs={{0,3},{1,0},{2,1},{3,2},{4,7},{5,4},{6,5},{7,6},{8,11},{9,8},{10,9... | collective-permute-start | bytes 1769480 | tf_op jit(solution)/shard_map/ppermute | solution.py:39
  7.0 5.0 %shard_map.102 = (bf16[256,3072]{1,0:T(8,128)(2,1)S(1)}, bf16[256,3072]{1,0:T(8,128)(2,1)S(1)}, f32[256,1]{1,0:T(8,128)S(1)}, bf16[256,128]{1,0:T(8,128)(2,1)S(1)}, bf16[256,256]{1,0:T(8,128)(2,1)S(1)}) custom-call(f32[1,3072]{1,0:T(1,128)S(1)} %bitcast.4, bf16[256,3072]{1,0:T(8,128)(2,1)} %rest_8_.3, bf16[256,3072]{1,0:T(8,128)(2,1)S(1)} %copy-done, ...), custom_call_target="tpu_custom_call" | custom-call | flops 5000000000 | tf_op jit(solution)/shard_map/pallas_call | solution.py:96
  12.0 0.8 shard_map.103
  13.5 1.1 %collective-permute-done.1.rest_0_ = bf16[384,512]{1,0:T(8,128)(2,1)S(1)} collective-permute-done((bf16[384,512]{1,0:T(8,128)(2,1)S(1)}, bf16[384,512]{1,0:T(8,128)(2,1)S(1)}, u32[]{:S(2)}, u32[]{:S(2)}) %collective-permute-start.1) | collective-permute-done | bytes 393248 | tf_op jit(solution)/shard_map/ppermute | solution.py:43
  16.0 9.0 %collective-permute-done.refs_0_ = bf16[768,384]{1,0:T(8,128)(2,1)S(1)} collective-permute-done((bf16[768,384]{1,0:T(8,128)(2,1)S(1)}, bf16[768,384]{1,0:T(8,128)(2,1)S(1)}, u32[]{:S(2)}, u32[]{:S(2)}) %collective-permute-start) | collective-permute-done | bytes 589856 | tf_op jit(solution)/shard_map/ppermute | solution.py:39
  25.0 1.8 %collective-permute-start.5 = (bf16[768,384]{1,0:T(8,128)(2,1)S(1)}, bf16[768,384]{1,0:T(8,128)(2,1)S(1)}, u32[]{:S(2)}, u32[]{:S(2)}) collective-permute-start(bf16[768,384]{1,0:T(8,128)(2,1)S(1)} %shard_map.105.rest_0_), channel_id=1, source_target_pairs={{0,128},{64,192},{128,0},{192,64},{1,129},{65,193},{129,1},{193,65... | collective-permute-start | bytes 1769480 | tf_op jit(solution)/shard_map/ppermute | solution.py:43
  26.8 12.8 %collective-permute-done.5.rest_1_ = bf16[768,384]{1,0:T(8,128)(2,1)S(1)} collective-permute-done((bf16[768,384]{1,0:T(8,128)(2,1)S(1)}, bf16[768,384]{1,0:T(8,128)(2,1)S(1)}, u32[]{:S(2)}, u32[]{:S(2)}) %collective-permute-start.5) | collective-permute-done | bytes 589856 | tf_op jit(solution)/shard_map/ppermute | solution.py:43
  39.6 1.7 %collective-permute-start.15 = (bf16[384,384]{1,0:T(8,128)(2,1)S(1)}, bf16[384,384]{1,0:T(8,128)(2,1)S(1)}, u32[]{:S(2)}, u32[]{:S(2)}) collective-permute-start(bf16[384,384]{1,0:T(8,128)(2,1)S(1)} %get-tuple-element.56.refs_1_.rest_4_), channel_id=1, source_target_pairs={{0,128},{64,192},{128,0},{192,64},{1,129},{65,193},{129,1},{193,65... | collective-permute-start | bytes 884744 | tf_op jit(solution)/shard_map/ppermute | solution.py:43
  41.3 2.7 %collective-permute-done.9.rest_6_.rest_1_.rest_5_ = bf16[768,384]{1,0:T(8,128)(2,1)S(1)} collective-permute-done((bf16[768,384]{1,0:T(8,128)(2,1)S(1)}, bf16[768,384]{1,0:T(8,128)(2,1)S(1)}, u32[]{:S(2)}, u32[]{:S(2)}) %collective-permute-start.9) | collective-permute-done | bytes 589856 | tf_op jit(solution)/shard_map/ppermute | solution.py:39
  44.0 1.2 %collective-permute-done.8.rest_5_.rest_0_.rest_4_ = bf16[768,384]{1,0:T(8,128)(2,1)S(1)} collective-permute-done((bf16[768,384]{1,0:T(8,128)(2,1)S(1)}, bf16[768,384]{1,0:T(8,128)(2,1)S(1)}, u32[]{:S(2)}, u32[]{:S(2)}) %collective-permute-start.8) | collective-permute-done | bytes 589856 | tf_op jit(solution)/shard_map/ppermute | solution.py:39
  45.3 1.8 %shard_map.106 = (bf16[256,128]{1,0:T(8,128)(2,1)S(1)}, bf16[256,256]{1,0:T(8,128)(2,1)S(1)}, bf16[384,512]{1,0:T(8,128)(2,1)S(1)}, bf16[384,512]{1,0:T(8,128)(2...) custom-call(s32[1]{0:T(128)} %bitcast.place_1.place_ref, bf16[256,3072]{1,0:T(8,128)(2,1)S(1)} %get-tuple-element.48.normed, ...), custom_call_target="tpu_custom_call" | custom-call | flops 4000000000 | tf_op jit(solution)/shard_map/pallas_call | solution.py:96
  47.1 0.6 collective-permute-start.12
  47.8 1.2 %collective-permute-done.15.refs_0_ = bf16[384,384]{1,0:T(8,128)(2,1)S(1)} collective-permute-done((bf16[384,384]{1,0:T(8,128)(2,1)S(1)}, bf16[384,384]{1,0:T(8,128)(2,1)S(1)}, u32[]{:S(2)}, u32[]{:S(2)}) %collective-permute-start.15) | collective-permute-done | bytes 294944 | tf_op jit(solution)/shard_map/ppermute | solution.py:43
  49.1 0.6 collective-permute-done.13.rest_1_
  49.6 1.1 %collective-permute-done.14.rest_2_ = bf16[384,512]{1,0:T(8,128)(2,1)S(1)} collective-permute-done((bf16[384,512]{1,0:T(8,128)(2,1)S(1)}, bf16[384,512]{1,0:T(8,128)(2,1)S(1)}, u32[]{:S(2)}, u32[]{:S(2)}) %collective-permute-start.14) | collective-permute-done | bytes 393248 | tf_op jit(solution)/shard_map/ppermute | solution.py:43
  51.0 1.8 %collective-permute-start.16 = (bf16[384,768]{1,0:T(8,128)(2,1)S(1)}, bf16[384,768]{1,0:T(8,128)(2,1)S(1)}, u32[]{:S(2)}, u32[]{:S(2)}) collective-permute-start(bf16[384,768]{1,0:T(8,128)(2,1)S(1)} %get-tuple-element.65), channel_id=1, source_target_pairs={{0,128},{64,192},{128,0},{192,64},{1,129},{65,193},{129,1},{193,65... | collective-permute-start | bytes 1769480 | tf_op jit(solution)/shard_map/ppermute | solution.py:43
  52.8 1.8 %shard_map.107 = (bf16[256,128]{1,0:T(8,128)(2,1)S(1)}, bf16[256,256]{1,0:T(8,128)(2,1)S(1)}, bf16[384,512]{1,0:T(8,128)(2,1)S(1)}, bf16[384,512]{1,0:T(8,128)(2...) custom-call(s32[1]{0:T(128)} %bitcast.1.place_2.place_ref, ...), custom_call_target="tpu_custom_call" | custom-call | flops 4000000000 | tf_op jit(solution)/shard_map/pallas_call | solution.py:96
  55.3 7.7 %shard_map.110 = (bf16[256,3072]{1,0:T(8,128)(2,1)}, f32[8,128]{1,0:T(8,128)S(1)}) custom-call(s32[1]{0:T(128)} %bitcast.place_1.place_ref, s32[1]{0:T(128)} %bitcast.1.place_2.place_ref, bf16[256,3072]{1,0:T(8,128)(2,1)S(1)} %get-tuple-element.49.cot, f32[1,3072]{1,0:T(1,128)S(1)} %bitcast.5, f32[256,1]{1,0:T(8,128)S(1)} %get-tuple-element.69.inverse_ref, ...), custom_call_target="tpu_custom_call" | custom-call | flops 5000000000 | tf_op jit(solution)/shard_map/pallas_call | solution.py:96
  63.1 3.3 %collective-permute-done.16.here_1 = bf16[384,768]{1,0:T(8,128)(2,1)S(1)} collective-permute-done((bf16[384,768]{1,0:T(8,128)(2,1)S(1)}, bf16[384,768]{1,0:T(8,128)(2,1)S(1)}, u32[]{:S(2)}, u32[]{:S(2)}) %collective-permute-start.16) | collective-permute-done | bytes 589856 | tf_op jit(solution)/shard_map/ppermute | solution.py:43
  66.7 1.8 %collective-permute-start.20 = (bf16[384,384]{1,0:T(8,128)(2,1)S(1)}, bf16[384,384]{1,0:T(8,128)(2,1)S(1)}, u32[]{:S(2)}, u32[]{:S(2)}) collective-permute-start(bf16[384,384]{1,0:T(8,128)(2,1)S(1)} %get-tuple-element.73.rest_10_), channel_id=1, source_target_pairs={{0,128},{64,192},{128,0},{192,64},{1,129},{65,193},{129,1},{193,65... | collective-permute-start | bytes 884744 | tf_op jit(solution)/shard_map/ppermute | solution.py:43
  68.6 2.1 %collective-permute-start.23 = (bf16[384,768]{1,0:T(8,128)(2,1)S(1)}, bf16[384,768]{1,0:T(8,128)(2,1)S(1)}, u32[]{:S(2)}, u32[]{:S(2)}) collective-permute-start(bf16[384,768]{1,0:T(8,128)(2,1)S(1)} %get-tuple-element.82), channel_id=1, source_target_pairs={{0,191},{1,0},{2,1},{3,2},{4,3},{5,4},{6,5},{7,6},{8,7},{9,8},{10,... | collective-permute-start | bytes 1769480 | tf_op jit(solution)/shard_map/ppermute | solution.py:39
  70.7 3.9 %shard_map.112 = (bf16[256,3072]{1,0:T(8,128)(2,1)}, f32[8,128]{1,0:T(8,128)S(1)}) custom-call(s32[1]{0:T(128)} %bitcast.place_1.place_ref, s32[1]{0:T(128)} %bitcast.1.place_2.place_ref, bf16[256,128]{1,0:T(8,128)(2,1)S(1)} %get-tuple-element.47.hidden.hidden_0, bf16[256,128]{1,0:T(8,128)(2,1)S(1)} %get-tuple-element.57.rest_4_.refs_1_.hidden_1, ...), custom_call_target="tpu_custom_call" | custom-call | flops 4000000000 | tf_op jit(solution)/shard_map/pallas_call | solution.py:96
  75.1 1.8 %collective-permute-start.21 = (bf16[384,384]{1,0:T(8,128)(2,1)S(1)}, bf16[384,384]{1,0:T(8,128)(2,1)S(1)}, u32[]{:S(2)}, u32[]{:S(2)}) collective-permute-start(bf16[384,384]{1,0:T(8,128)(2,1)S(1)} %get-tuple-element.81), channel_id=1, source_target_pairs={{0,128},{64,192},{128,0},{192,64},{1,129},{65,193},{129,1},{193,65... | collective-permute-start | bytes 884744 | tf_op jit(solution)/shard_map/ppermute | solution.py:43
  76.9 1.7 %collective-permute-start.24 = (bf16[384,384]{1,0:T(8,128)(2,1)S(1)}, bf16[384,384]{1,0:T(8,128)(2,1)S(1)}, u32[]{:S(2)}, u32[]{:S(2)}) collective-permute-start(bf16[384,384]{1,0:T(8,128)(2,1)S(1)} %get-tuple-element.83), channel_id=1, source_target_pairs={{0,190},{1,191},{2,0},{3,1},{4,2},{5,3},{6,4},{7,5},{8,6},{9,7},{1... | collective-permute-start | bytes 884744 | tf_op jit(solution)/shard_map/ppermute | solution.py:39
  78.6 3.9 %collective-permute-done.21.arrived = bf16[384,384]{1,0:T(8,128)(2,1)S(1)} collective-permute-done((bf16[384,384]{1,0:T(8,128)(2,1)S(1)}, bf16[384,384]{1,0:T(8,128)(2,1)S(1)}, u32[]{:S(2)}, u32[]{:S(2)}) %collective-permute-start.21) | collective-permute-done | bytes 294944 | tf_op jit(solution)/shard_map/ppermute | solution.py:43
  82.6 2.3 %collective-permute-start.25 = (bf16[384,384]{1,0:T(8,128)(2,1)S(1)}, bf16[384,384]{1,0:T(8,128)(2,1)S(1)}, u32[]{:S(2)}, u32[]{:S(2)}) collective-permute-start(bf16[384,384]{1,0:T(8,128)(2,1)S(1)} %shard_map.114.refs_1_), channel_id=1, source_target_pairs={{0,190},{1,191},{2,0},{3,1},{4,2},{5,3},{6,4},{7,5},{8,6},{9,7},{1... | collective-permute-start | bytes 884744 | tf_op jit(solution)/shard_map/ppermute | solution.py:39
  84.9 1.8 %collective-permute-start.22 = (bf16[384,384]{1,0:T(8,128)(2,1)S(1)}, bf16[384,384]{1,0:T(8,128)(2,1)S(1)}, u32[]{:S(2)}, u32[]{:S(2)}) collective-permute-start(bf16[384,384]{1,0:T(8,128)(2,1)S(1)} %shard_map.115), channel_id=1, source_target_pairs={{0,128},{64,192},{128,0},{192,64},{1,129},{65,193},{129,1},{193,65... | collective-permute-start | bytes 884744 | tf_op jit(solution)/shard_map/ppermute | solution.py:43
  86.7 8.8 %collective-permute-done.23.refs_0_ = bf16[384,768]{1,0:T(8,128)(2,1)S(1)} collective-permute-done((bf16[384,768]{1,0:T(8,128)(2,1)S(1)}, bf16[384,768]{1,0:T(8,128)(2,1)S(1)}, u32[]{:S(2)}, u32[]{:S(2)}) %collective-permute-start.23) | collective-permute-done | bytes 589856 | tf_op jit(solution)/shard_map/ppermute | solution.py:39
  95.5 2.3 %collective-permute-done.25.high = bf16[384,384]{1,0:T(8,128)(2,1)S(1)} collective-permute-done((bf16[384,384]{1,0:T(8,128)(2,1)S(1)}, bf16[384,384]{1,0:T(8,128)(2,1)S(1)}, u32[]{:S(2)}, u32[]{:S(2)}) %collective-permute-start.25) | collective-permute-done | bytes 294944 | tf_op jit(solution)/shard_map/ppermute | solution.py:39
  97.7 1.3 %shard_map.117 = (f32[768,128]{1,0:T(8,128)}, f32[768,128]{1,0:T(8,128)}, f32[128,768]{1,0:T(8,128)}) custom-call(f32[384,768]{1,0:T(8,128)S(1)} %get-tuple-element.76.mine, bf16[384,384]{1,0:T(8,128)(2,1)S(1)} %shard_map.108.rest_3_.here_low, bf16[384,384]{1,0:T(8,128)(2,1)S(1)} %collective-permute-done.22.here_high, bf16[384,768]{1,0:T(8,128)(2,1)S(1)} %shard_map.116.near, ...), custom_call_target="tpu_custom_call" | custom-call | flops 2000000000 | tf_op jit(solution)/shard_map/pallas_call | solution.py:96
  (41 shorter events, 4.1 us)
Async XLA Ops:
  0.7 6.4 %copy-start = (bf16[256,3072]{1,0:T(8,128)(2,1)S(1)}, bf16[256,3072]{1,0:T(8,128)(2,1)}, u32[]{:S(2)}) copy-start(bf16[256,3072]{1,0:T(8,128)(2,1)} %cot_far.1) | copy-start | bytes 4718596
  0.7 6.4 %copy-start.1 = (f32[3072]{0:T(1024)S(1)}, f32[3072]{0:T(1024)}, u32[]{:S(2)}) copy-start(f32[3072]{0:T(1024)} %param.8) | copy-start | bytes 36868
  2.4 22.6 %collective-permute-start = (bf16[768,384]{1,0:T(8,128)(2,1)S(1)}, bf16[768,384]{1,0:T(8,128)(2,1)S(1)}, u32[]{:S(2)}, u32[]{:S(2)}) collective-permute-start(bf16[768,384]{1,0:T(8,128)(2,1)S(1)} %get-tuple-element.50), channel_id=1, source_target_pairs={{0,1},{1,2},{2,3},{3,4},{4,5},{5,6},{6,7},{7,8},{8,9},{9,10},{10,1... | collective-permute-start | bytes 1769480 | tf_op jit(solution)/shard_map/ppermute | solution.py:39
  4.0 21.0 %collective-permute-start.4 = (bf16[768,384]{1,0:T(8,128)(2,1)S(1)}, bf16[768,384]{1,0:T(8,128)(2,1)S(1)}, u32[]{:S(2)}, u32[]{:S(2)}) collective-permute-start(bf16[768,384]{1,0:T(8,128)(2,1)S(1)} %get-tuple-element.46.rest_0_), channel_id=1, source_target_pairs={{0,3},{1,0},{2,1},{3,2},{4,7},{5,4},{6,5},{7,6},{8,11},{9,8},{10,9... | collective-permute-start | bytes 1769480 | tf_op jit(solution)/shard_map/ppermute | solution.py:39
  12.8 1.8 %collective-permute-start.1 = (bf16[384,512]{1,0:T(8,128)(2,1)S(1)}, bf16[384,512]{1,0:T(8,128)(2,1)S(1)}, u32[]{:S(2)}, u32[]{:S(2)}) collective-permute-start(bf16[384,512]{1,0:T(8,128)(2,1)S(1)} %get-tuple-element.53), channel_id=1, source_target_pairs={{0,64},{64,0},{128,192},{192,128},{1,65},{65,1},{129,193},{193,129... | collective-permute-start | bytes 1179656 | tf_op jit(solution)/shard_map/ppermute | solution.py:43
  12.9 2.3 %collective-permute-start.2 = (bf16[384,512]{1,0:T(8,128)(2,1)S(1)}, bf16[384,512]{1,0:T(8,128)(2,1)S(1)}, u32[]{:S(2)}, u32[]{:S(2)}) collective-permute-start(bf16[384,512]{1,0:T(8,128)(2,1)S(1)} %get-tuple-element.54), channel_id=1, source_target_pairs={{0,64},{64,0},{128,192},{192,128},{1,65},{65,1},{129,193},{193,129... | collective-permute-start | bytes 1179656 | tf_op jit(solution)/shard_map/ppermute | solution.py:43
  13.4 2.3 %collective-permute-start.3 = (bf16[384,512]{1,0:T(8,128)(2,1)S(1)}, bf16[384,512]{1,0:T(8,128)(2,1)S(1)}, u32[]{:S(2)}, u32[]{:S(2)}) collective-permute-start(bf16[384,512]{1,0:T(8,128)(2,1)S(1)} %get-tuple-element.55), channel_id=1, source_target_pairs={{0,64},{64,0},{128,192},{192,128},{1,65},{65,1},{129,193},{193,129... | collective-permute-start | bytes 1179656 | tf_op jit(solution)/shard_map/ppermute | solution.py:43
  25.0 14.6 %collective-permute-start.5 = (bf16[768,384]{1,0:T(8,128)(2,1)S(1)}, bf16[768,384]{1,0:T(8,128)(2,1)S(1)}, u32[]{:S(2)}, u32[]{:S(2)}) collective-permute-start(bf16[768,384]{1,0:T(8,128)(2,1)S(1)} %shard_map.105.rest_0_), channel_id=1, source_target_pairs={{0,128},{64,192},{128,0},{192,64},{1,129},{65,193},{129,1},{193,65... | collective-permute-start | bytes 1769480 | tf_op jit(solution)/shard_map/ppermute | solution.py:43
  26.8 17.2 %collective-permute-start.9 = (bf16[768,384]{1,0:T(8,128)(2,1)S(1)}, bf16[768,384]{1,0:T(8,128)(2,1)S(1)}, u32[]{:S(2)}, u32[]{:S(2)}) collective-permute-start(bf16[768,384]{1,0:T(8,128)(2,1)S(1)} %collective-permute-done.4.refs_2_), channel_id=1, source_target_pairs={{0,3},{1,4},{2,5},{3,2},{4,7},{5,8},{6,9},{7,6},{8,11},{9,12},{10,... | collective-permute-start | bytes 1769480 | tf_op jit(solution)/shard_map/ppermute | solution.py:39
  26.8 18.5 %collective-permute-start.8 = (bf16[768,384]{1,0:T(8,128)(2,1)S(1)}, bf16[768,384]{1,0:T(8,128)(2,1)S(1)}, u32[]{:S(2)}, u32[]{:S(2)}) collective-permute-start(bf16[768,384]{1,0:T(8,128)(2,1)S(1)} %shard_map.105.rest_0_), channel_id=1, source_target_pairs={{0,1},{1,2},{2,3},{3,4},{4,5},{5,6},{6,7},{7,8},{8,9},{9,10},{10,1... | collective-permute-start | bytes 1769480 | tf_op jit(solution)/shard_map/ppermute | solution.py:39
  26.8 18.5 %collective-permute-start.6 = (bf16[768,384]{1,0:T(8,128)(2,1)S(1)}, bf16[768,384]{1,0:T(8,128)(2,1)S(1)}, u32[]{:S(2)}, u32[]{:S(2)}) collective-permute-start(bf16[768,384]{1,0:T(8,128)(2,1)S(1)} %shard_map.105.rest_0_), channel_id=1, source_target_pairs={{0,64},{64,0},{128,192},{192,128},{1,65},{65,1},{129,193},{193,129... | collective-permute-start | bytes 1769480 | tf_op jit(solution)/shard_map/ppermute | solution.py:43
  39.6 5.7 %collective-permute-start.7 = (bf16[768,384]{1,0:T(8,128)(2,1)S(1)}, bf16[768,384]{1,0:T(8,128)(2,1)S(1)}, u32[]{:S(2)}, u32[]{:S(2)}) collective-permute-start(bf16[768,384]{1,0:T(8,128)(2,1)S(1)} %collective-permute-done.5.rest_1_), channel_id=1, source_target_pairs={{0,64},{64,0},{128,192},{192,128},{1,65},{65,1},{129,193},{193,129... | collective-permute-start | bytes 1769480 | tf_op jit(solution)/shard_map/ppermute | solution.py:43
  39.6 9.4 %collective-permute-start.15 = (bf16[384,384]{1,0:T(8,128)(2,1)S(1)}, bf16[384,384]{1,0:T(8,128)(2,1)S(1)}, u32[]{:S(2)}, u32[]{:S(2)}) collective-permute-start(bf16[384,384]{1,0:T(8,128)(2,1)S(1)} %get-tuple-element.56.refs_1_.rest_4_), channel_id=1, source_target_pairs={{0,128},{64,192},{128,0},{192,64},{1,129},{65,193},{129,1},{193,65... | collective-permute-start | bytes 884744 | tf_op jit(solution)/shard_map/ppermute | solution.py:43
  44.0 8.8 %collective-permute-start.11 = (bf16[768,384]{1,0:T(8,128)(2,1)S(1)}, bf16[768,384]{1,0:T(8,128)(2,1)S(1)}, u32[]{:S(2)}, u32[]{:S(2)}) collective-permute-start(bf16[768,384]{1,0:T(8,128)(2,1)S(1)} %collective-permute-done.9.rest_6_.rest_1_.rest_5_), channel_id=1, source_target_pairs={{0,64},{64,0},{128,192},{192,128},{1,65},{65,1},{129,193},{193,129... | collective-permute-start | bytes 1769480 | tf_op jit(solution)/shard_map/ppermute | solution.py:43
  45.3 7.5 %collective-permute-start.10 = (bf16[768,384]{1,0:T(8,128)(2,1)S(1)}, bf16[768,384]{1,0:T(8,128)(2,1)S(1)}, u32[]{:S(2)}, u32[]{:S(2)}) collective-permute-start(bf16[768,384]{1,0:T(8,128)(2,1)S(1)} %collective-permute-done.8.rest_5_.rest_0_.rest_4_), channel_id=1, source_target_pairs={{0,64},{64,0},{128,192},{192,128},{1,65},{65,1},{129,193},{193,129... | collective-permute-start | bytes 1769480 | tf_op jit(solution)/shard_map/ppermute | solution.py:43
  47.1 2.0 %collective-permute-start.12 = (bf16[384,512]{1,0:T(8,128)(2,1)S(1)}, bf16[384,512]{1,0:T(8,128)(2,1)S(1)}, u32[]{:S(2)}, u32[]{:S(2)}) collective-permute-start(bf16[384,512]{1,0:T(8,128)(2,1)S(1)} %get-tuple-element.61), channel_id=1, source_target_pairs={{0,64},{64,0},{128,192},{192,128},{1,65},{65,1},{129,193},{193,129... | collective-permute-start | bytes 1179656 | tf_op jit(solution)/shard_map/ppermute | solution.py:43
  47.7 1.9 %collective-permute-start.13 = (bf16[384,512]{1,0:T(8,128)(2,1)S(1)}, bf16[384,512]{1,0:T(8,128)(2,1)S(1)}, u32[]{:S(2)}, u32[]{:S(2)}) collective-permute-start(bf16[384,512]{1,0:T(8,128)(2,1)S(1)} %get-tuple-element.62), channel_id=1, source_target_pairs={{0,64},{64,0},{128,192},{192,128},{1,65},{65,1},{129,193},{193,129... | collective-permute-start | bytes 1179656 | tf_op jit(solution)/shard_map/ppermute | solution.py:43
  49.0 1.7 %collective-permute-start.14 = (bf16[384,512]{1,0:T(8,128)(2,1)S(1)}, bf16[384,512]{1,0:T(8,128)(2,1)S(1)}, u32[]{:S(2)}, u32[]{:S(2)}) collective-permute-start(bf16[384,512]{1,0:T(8,128)(2,1)S(1)} %get-tuple-element.63), channel_id=1, source_target_pairs={{0,64},{64,0},{128,192},{192,128},{1,65},{65,1},{129,193},{193,129... | collective-permute-start | bytes 1179656 | tf_op jit(solution)/shard_map/ppermute | solution.py:43
  51.0 15.5 %collective-permute-start.16 = (bf16[384,768]{1,0:T(8,128)(2,1)S(1)}, bf16[384,768]{1,0:T(8,128)(2,1)S(1)}, u32[]{:S(2)}, u32[]{:S(2)}) collective-permute-start(bf16[384,768]{1,0:T(8,128)(2,1)S(1)} %get-tuple-element.65), channel_id=1, source_target_pairs={{0,128},{64,192},{128,0},{192,64},{1,129},{65,193},{129,1},{193,65... | collective-permute-start | bytes 1769480 | tf_op jit(solution)/shard_map/ppermute | solution.py:43
  54.6 8.4 %collective-permute-start.17 = (bf16[384,512]{1,0:T(8,128)(2,1)S(1)}, bf16[384,512]{1,0:T(8,128)(2,1)S(1)}, u32[]{:S(2)}, u32[]{:S(2)}) collective-permute-start(bf16[384,512]{1,0:T(8,128)(2,1)S(1)} %get-tuple-element.66), channel_id=1, source_target_pairs={{0,64},{64,0},{128,192},{192,128},{1,65},{65,1},{129,193},{193,129... | collective-permute-start | bytes 1179656 | tf_op jit(solution)/shard_map/ppermute | solution.py:43
  54.7 8.3 %collective-permute-start.18 = (bf16[384,512]{1,0:T(8,128)(2,1)S(1)}, bf16[384,512]{1,0:T(8,128)(2,1)S(1)}, u32[]{:S(2)}, u32[]{:S(2)}) collective-permute-start(bf16[384,512]{1,0:T(8,128)(2,1)S(1)} %get-tuple-element.67), channel_id=1, source_target_pairs={{0,64},{64,0},{128,192},{192,128},{1,65},{65,1},{129,193},{193,129... | collective-permute-start | bytes 1179656 | tf_op jit(solution)/shard_map/ppermute | solution.py:43
  55.2 7.8 %collective-permute-start.19 = (bf16[384,512]{1,0:T(8,128)(2,1)S(1)}, bf16[384,512]{1,0:T(8,128)(2,1)S(1)}, u32[]{:S(2)}, u32[]{:S(2)}) collective-permute-start(bf16[384,512]{1,0:T(8,128)(2,1)S(1)} %get-tuple-element.68), channel_id=1, source_target_pairs={{0,64},{64,0},{128,192},{192,128},{1,65},{65,1},{129,193},{193,129... | collective-permute-start | bytes 1179656 | tf_op jit(solution)/shard_map/ppermute | solution.py:43
  66.7 8.3 %collective-permute-start.20 = (bf16[384,384]{1,0:T(8,128)(2,1)S(1)}, bf16[384,384]{1,0:T(8,128)(2,1)S(1)}, u32[]{:S(2)}, u32[]{:S(2)}) collective-permute-start(bf16[384,384]{1,0:T(8,128)(2,1)S(1)} %get-tuple-element.73.rest_10_), channel_id=1, source_target_pairs={{0,128},{64,192},{128,0},{192,64},{1,129},{65,193},{129,1},{193,65... | collective-permute-start | bytes 884744 | tf_op jit(solution)/shard_map/ppermute | solution.py:43
  68.6 26.9 %collective-permute-start.23 = (bf16[384,768]{1,0:T(8,128)(2,1)S(1)}, bf16[384,768]{1,0:T(8,128)(2,1)S(1)}, u32[]{:S(2)}, u32[]{:S(2)}) collective-permute-start(bf16[384,768]{1,0:T(8,128)(2,1)S(1)} %get-tuple-element.82), channel_id=1, source_target_pairs={{0,191},{1,0},{2,1},{3,2},{4,3},{5,4},{6,5},{7,6},{8,7},{9,8},{10,... | collective-permute-start | bytes 1769480 | tf_op jit(solution)/shard_map/ppermute | solution.py:39
  75.1 7.4 %collective-permute-start.21 = (bf16[384,384]{1,0:T(8,128)(2,1)S(1)}, bf16[384,384]{1,0:T(8,128)(2,1)S(1)}, u32[]{:S(2)}, u32[]{:S(2)}) collective-permute-start(bf16[384,384]{1,0:T(8,128)(2,1)S(1)} %get-tuple-element.81), channel_id=1, source_target_pairs={{0,128},{64,192},{128,0},{192,64},{1,129},{65,193},{129,1},{193,65... | collective-permute-start | bytes 884744 | tf_op jit(solution)/shard_map/ppermute | solution.py:43
  76.9 18.5 %collective-permute-start.24 = (bf16[384,384]{1,0:T(8,128)(2,1)S(1)}, bf16[384,384]{1,0:T(8,128)(2,1)S(1)}, u32[]{:S(2)}, u32[]{:S(2)}) collective-permute-start(bf16[384,384]{1,0:T(8,128)(2,1)S(1)} %get-tuple-element.83), channel_id=1, source_target_pairs={{0,190},{1,191},{2,0},{3,1},{4,2},{5,3},{6,4},{7,5},{8,6},{9,7},{1... | collective-permute-start | bytes 884744 | tf_op jit(solution)/shard_map/ppermute | solution.py:39
  82.6 15.2 %collective-permute-start.25 = (bf16[384,384]{1,0:T(8,128)(2,1)S(1)}, bf16[384,384]{1,0:T(8,128)(2,1)S(1)}, u32[]{:S(2)}, u32[]{:S(2)}) collective-permute-start(bf16[384,384]{1,0:T(8,128)(2,1)S(1)} %shard_map.114.refs_1_), channel_id=1, source_target_pairs={{0,190},{1,191},{2,0},{3,1},{4,2},{5,3},{6,4},{7,5},{8,6},{9,7},{1... | collective-permute-start | bytes 884744 | tf_op jit(solution)/shard_map/ppermute | solution.py:39
  84.9 10.6 %collective-permute-start.22 = (bf16[384,384]{1,0:T(8,128)(2,1)S(1)}, bf16[384,384]{1,0:T(8,128)(2,1)S(1)}, u32[]{:S(2)}, u32[]{:S(2)}) collective-permute-start(bf16[384,384]{1,0:T(8,128)(2,1)S(1)} %shard_map.115), channel_id=1, source_target_pairs={{0,128},{64,192},{128,0},{192,64},{1,129},{65,193},{129,1},{193,65... | collective-permute-start | bytes 884744 | tf_op jit(solution)/shard_map/ppermute | solution.py:43
